TPU v7x, 512 devices: a whole 4x4x16 slice. The times are simulated.
512 devices in a mesh: tm: 16 (over y, x), space: 32 (over z, core).
Axes of the slice: x: 4, y: 4, z: 16, core: 2. Of those that a mesh axis runs over, the one named last changes fastest.
Arguments:
- source: float32 [32, 8192, 128], P('tm', 'space'), may hold values from -6 to 6
- elem_scale: float32 [8192], P('space'), may hold values from 1 to 2
- diag_block: float32 [128, 128], replicated, as said below
- block_inverse: float32 [128, 128], replicated, as said below
- face_flux: float32 [4, 128, 128], replicated, may hold values from -0.072 to 0.072
- time_trace: float32 [128, 128], replicated, as said below
- neighbours: int32 [8192, 4], P('space'), may hold values from 0 to 287, as said below
- send_rows: int32 [32, 32], P('space'), may hold values from 0 to 255, as said below
Outputs:
- smoothed: float32 [32, 8192, 128], P('tm', 'space')
Inputs may be any that keep to these rules, and one draw needn't show every extreme that they name: `neighbours`: indexes the extended list of the element's own partition, of 288 positions; each of the 32 received positions is named by exactly one face of the partition's elements, and only the partition's sent elements name received positions. `send_rows`: each row holds 32 distinct local positions of its partition's elements. `diag_block`: the identity plus a skew-symmetric matrix plus a positive semidefinite matrix. `block_inverse`: the inverse of diag_block. `time_trace`: its largest singular value is at most 0.9.
All inputs are finite; a program needn't handle non-finite values.
Results may differ from a plain program's by a relative error of at most 0.0001.
Values sent between devices are 32-bit elements; how exact they have to be, the bound alone decides.
A program may use at most 64 MiB of HBM per device.

v0:
```python
import jax
import jax.numpy as jnp
from jax import lax
from jax.sharding import PartitionSpec as P

DAMPING = 0.7


def with_halo(block, sides, width):
    for axis, dim in sides:
        count = lax.axis_size(axis)
        forward = [(i, i + 1) for i in range(count - 1)]
        forward.append((count - 1, 0))
        backward = [(target, source) for source, target in forward]
        low = lax.ppermute(
            lax.slice_in_dim(block, block.shape[dim] - width, None, axis=dim), axis, forward
        )
        high = lax.ppermute(lax.slice_in_dim(block, 0, width, axis=dim), axis, backward)
        block = jnp.concatenate([low, block, high], axis=dim)
    return block


def passed_along(x, axis, by):
    length = lax.axis_size(axis)
    pairs = [(i, i + by) for i in range(length) if 0 <= i + by < length]
    return lax.ppermute(x, axis, pairs)


def entering(value, axis, join, neutral):
    count, mine = (lax.axis_size(axis), lax.axis_index(axis))
    pieces = jax.tree.map(lambda part: lax.all_gather(part, axis), value)
    running = jax.tree.map(
        lambda part, zero: jnp.full_like(part, 0) + jnp.asarray(zero, part.dtype), value, neutral
    )

    def turn(position, running):
        longer = join(running, jax.tree.map(lambda part: part[position], pieces))
        return jax.tree.map(lambda new, old: jnp.where(position < mine, new, old), longer, running)

    return lax.fori_loop(0, count - 1, turn, running)


def product(left, right):
    return jnp.dot(left, right, precision=lax.Precision.HIGHEST, preferred_element_type=jnp.float32)


def body(
    source, elem_scale, diag_block, block_inverse, face_flux, time_trace, neighbours, send_rows
):
    slab_count, elements, unknowns = source.shape
    send_order = send_rows[0]
    halo_rows = send_order.shape[0] // 2
    inv_scale = 1.0 / elem_scale
    coarse_scale = 1.0 / (2.0 * elem_scale - 1.0)
    coarse_count = slab_count // 2

    def operate(field):
        outgoing = field[:, send_order, :]
        padded = with_halo(outgoing, (("space", 1),), halo_rows)
        extended = jnp.concatenate(
            [field, padded[:, :halo_rows], padded[:, 3 * halo_rows :]], axis=1
        )
        face_term = jnp.zeros((slab_count * elements, unknowns), jnp.float32)
        for face_index in range(4):
            picked = jnp.take(extended, neighbours[:, face_index], axis=1)
            face_term = face_term + product(picked.reshape(-1, unknowns), face_flux[face_index])
        incoming = passed_along(field[-1], "tm", 1)
        earlier = jnp.concatenate([incoming[None], field[:-1]], axis=0)
        diagonal_term = (
            product(field.reshape(-1, unknowns), diag_block).reshape(field.shape)
            * elem_scale[None, :, None]
        )
        time_term = product(earlier.reshape(-1, unknowns), time_trace).reshape(field.shape)
        return diagonal_term - time_term - face_term.reshape(field.shape)

    def precondition(residual):
        return (
            product(residual.reshape(-1, unknowns), block_inverse).reshape(residual.shape)
            * inv_scale[None, :, None]
        )

    def smooth(solution):
        return solution + DAMPING * precondition(source - operate(solution))

    def coarse_step(state, rhs_slab):
        state = coarse_scale[:, None] * product(
            rhs_slab + product(state, time_trace), block_inverse
        )
        return (state, state)

    def run_chain(start_state, coarse_rhs):
        final_state, every_state = lax.scan(coarse_step, start_state, coarse_rhs)
        return every_state

    solution = DAMPING * precondition(source)
    solution = smooth(solution)
    residual = source - operate(solution)
    paired = residual.reshape(coarse_count, 2, elements, unknowns)
    coarse_rhs = paired[:, 0] + paired[:, 1]
    zero_state = jnp.zeros((elements, unknowns), jnp.float32)
    offset = run_chain(zero_state, coarse_rhs)[-1]
    propagator = product(time_trace, block_inverse)

    def power_step(step_index, matrix_power):
        return product(matrix_power, propagator)

    matrix_power = lax.fori_loop(0, coarse_count - 1, power_step, propagator)
    factor = coarse_scale**coarse_count

    def combine(earlier_map, later_map):
        mat_early, fac_early, off_early = earlier_map
        mat_late, fac_late, off_late = later_map
        return (
            product(mat_early, mat_late),
            fac_early * fac_late,
            fac_late[:, None] * product(off_early, mat_late) + off_late,
        )

    identity = (
        jnp.eye(unknowns, dtype=jnp.float32),
        jnp.ones((elements,), jnp.float32),
        jnp.zeros((elements, unknowns), jnp.float32),
    )
    prefix = entering((matrix_power, factor, offset), "tm", combine, identity)
    correction = run_chain(prefix[2], coarse_rhs)
    solution = solution + jnp.repeat(correction, 2, axis=0)
    solution = smooth(solution)
    solution = smooth(solution)
    return solution


def solution(mesh):
    in_specs = (
        P("tm", "space", None),
        P("space"),
        P(),
        P(),
        P(),
        P(),
        P("space", None),
        P("space", None),
    )
    out_specs = P("tm", "space", None)
    return jax.shard_map(body, mesh=mesh, in_specs=in_specs, out_specs=out_specs, check_vma=False)
```

profile of v0, /device:TPU:1, one launch (start us, length us, event | category | flops | bytes accessed | tf_op | source)
XLA Modules:
  0.0 214.7 jit_solution(2782848406083276022)
XLA Ops:
  7.4 1.3 fusion.25
  10.2 3.0 %collective-permute-start.1 = (f32[2,16,128]{2,1,0:T(8,128)S(1)}, f32[2,16,128]{2,1,0:T(8,128)S(1)}, u32[]{:S(2)}, u32[]{:S(2)}) collective-permute-start(f32[2,16,128]{2,1,0:T(8,128)S(1)} %get-tuple-element.229), channel_id=1, source_target_pairs={{0,1},{1,2},{2,3},{3,4},{4,5},{5,6},{6,7},{7,8},{8,9},{9,10},{10,1... | collective-permute-start | bytes 49160 | tf_op jit(solution)/shard_map/ppermute | solution.py:15
  13.2 3.9 %collective-permute-start.2 = (f32[2,16,128]{2,1,0:T(8,128)S(1)}, f32[2,16,128]{2,1,0:T(8,128)S(1)}, u32[]{:S(2)}, u32[]{:S(2)}) collective-permute-start(f32[2,16,128]{2,1,0:T(8,128)S(1)} %get-tuple-element.230), channel_id=1, source_target_pairs={{1,0},{2,1},{3,2},{4,3},{5,4},{6,5},{7,6},{8,7},{9,8},{10,9},{11,1... | collective-permute-start | bytes 49160 | tf_op jit(solution)/shard_map/ppermute | solution.py:18
  17.1 1.3 collective-permute-start
  18.4 1.7 fusion.100
  21.1 1.0 gather_fusion.4
  30.0 5.7 %collective-permute-start.5 = (f32[2,16,128]{2,1,0:T(8,128)S(1)}, f32[2,16,128]{2,1,0:T(8,128)S(1)}, u32[]{:S(2)}, u32[]{:S(2)}) collective-permute-start(f32[2,16,128]{2,1,0:T(8,128)S(1)} %get-tuple-element.228), channel_id=1, source_target_pairs={{1,0},{2,1},{3,2},{4,3},{5,4},{6,5},{7,6},{8,7},{9,8},{10,9},{11,1... | collective-permute-start | bytes 49160 | tf_op jit(solution)/shard_map/ppermute | solution.py:18
  35.7 3.3 %collective-permute-start.3 = (f32[256,128]{1,0:T(8,128)S(1)}, f32[256,128]{1,0:T(8,128)S(1)}, u32[]{:S(2)}, u32[]{:S(2)}) collective-permute-start(f32[256,128]{1,0:T(8,128)S(1)} %get-tuple-element.219), channel_id=1, source_target_pairs={{0,32},{32,64},{64,96},{96,128},{128,160},{160,192},{192,224},{224... | collective-permute-start | bytes 393224 | tf_op jit(solution)/shard_map/ppermute | solution.py:26
  47.6 18.1 %all-gather.3 = f32[16,1,256]{2,1,0:T(1,128)S(1)} all-gather(f32[1,1,256]{2,1,0:T(1,128)S(1)} %bitcast.245), channel_id=2, replica_groups=mesh['tm'=16,'space'=32] {'tm'}, dimensions={0}, use_global_device_ids=true | all-gather | bytes 17408 | tf_op jit(solution)/shard_map/all_gather | solution.py:31
  65.7 14.3 %all-gather.7.cloned.1.call-done = f32[2048,128]{1,0:T(8,128)} async-done(((f32[128,128]{1,0:T(8,128)}), f32[2048,128]{1,0:T(8,128)}) %all-gather.7.cloned.1.call-update) | async-done | bytes 1048592 | tf_op jit(solution)/shard_map/all_gather | solution.py:31
  80.0 63.2 %all-gather.9.cloned.1.call-done = f32[4096,128]{1,0:T(8,128)} async-done(((f32[256,128]{1,0:T(8,128)}), f32[4096,128]{1,0:T(8,128)}) %all-gather.9.cloned.1.call-update) | async-done | bytes 2097168 | tf_op jit(solution)/shard_map/all_gather | solution.py:31
  143.3 33.7 %while.9 = (s32[]{:T(128)}, f32[256,128]{0,1:T(8,128)S(1)}, s32[]{:T(128)}, f32[16,256]{1,0:T(8,128)S(1)}, f32[16,128,128]{2,1,0:T(8,128)}, /*index=5*/f32[16,256,128]{2,1,0:T(8,128)}, s32[]{:T(128)}, s32[]{:T(128)}) while((s32[]{:T(128)}, f32[256,128]{0,1:T(8,128)S(1)}, s32[]{:T(128)}, f32[16,256]{1,0:T(8,128)S(1)}, ...), condition=%wide.region_2.4_spmd.clone, body=%wide.region_1.3_spmd.clone.sunk | while | flops 50495492 | bytes 1381487 | solution.py:40
  144.3 1.2 fusion.137
  146.6 1.2 fusion.137
  148.8 1.2 fusion.137
  151.1 1.2 fusion.137
  153.3 1.2 fusion.137
  155.6 1.2 fusion.137
  157.8 1.2 fusion.137
  160.1 1.2 fusion.137
  162.3 1.2 fusion.137
  164.6 1.2 fusion.137
  166.8 1.2 fusion.137
  169.1 1.2 fusion.137
  171.3 1.2 fusion.137
  173.6 1.2 fusion.137
  175.8 1.2 fusion.137
  178.9 2.7 %collective-permute-start.7 = (f32[2,16,128]{2,1,0:T(8,128)S(1)}, f32[2,16,128]{2,1,0:T(8,128)S(1)}, u32[]{:S(2)}, u32[]{:S(2)}) collective-permute-start(f32[2,16,128]{2,1,0:T(8,128)S(1)} %get-tuple-element.225), channel_id=1, source_target_pairs={{0,1},{1,2},{2,3},{3,4},{4,5},{5,6},{6,7},{7,8},{8,9},{9,10},{10,1... | collective-permute-start | bytes 49160 | tf_op jit(solution)/shard_map/ppermute | solution.py:15
  181.6 3.0 %collective-permute-start.6 = (f32[256,128]{1,0:T(8,128)S(1)}, f32[256,128]{1,0:T(8,128)S(1)}, u32[]{:S(2)}, u32[]{:S(2)}) collective-permute-start(f32[256,128]{1,0:T(8,128)S(1)} %get-tuple-element.217), channel_id=1, source_target_pairs={{0,32},{32,64},{64,96},{96,128},{128,160},{160,192},{192,224},{224... | collective-permute-start | bytes 393224 | tf_op jit(solution)/shard_map/ppermute | solution.py:26
  193.9 1.9 collective-permute-start.10
  195.9 2.5 %collective-permute-start.9 = (f32[256,128]{1,0:T(8,128)S(1)}, f32[256,128]{1,0:T(8,128)S(1)}, u32[]{:S(2)}, u32[]{:S(2)}) collective-permute-start(f32[256,128]{1,0:T(8,128)S(1)} %get-tuple-element.215), channel_id=1, source_target_pairs={{0,32},{32,64},{64,96},{96,128},{128,160},{160,192},{192,224},{224... | collective-permute-start | bytes 393224 | tf_op jit(solution)/shard_map/ppermute | solution.py:26
  206.8 1.1 fusion.11
  (217 shorter events, 54.0 us)
Async XLA Ops:
  6.5 0.8 copy-start
  6.5 13.9 %copy-start.5 = (f32[256]{0:T(256)S(1)}, f32[256]{0:T(256)}, u32[]{:S(2)}) copy-start(f32[256]{0:T(256)} %param.13) | copy-start | bytes 3076
  6.5 13.8 %copy-start.3 = (f32[128,128]{1,0:T(8,128)S(1)}, f32[128,128]{1,0:T(8,128)}, u32[]{:S(2)}) copy-start(f32[128,128]{1,0:T(8,128)} %param.17) | copy-start | bytes 196612
  6.5 13.7 %copy-start.6 = (s32[256,4]{0,1:T(4,128)S(1)}, s32[256,4]{0,1:T(4,128)}, u32[]{:S(2)}) copy-start(s32[256,4]{0,1:T(4,128)} %param.18) | copy-start | bytes 12292
  6.5 13.9 %copy-start.4 = (f32[128,128]{1,0:T(8,128)S(1)}, f32[128,128]{1,0:T(8,128)}, u32[]{:S(2)}) copy-start(f32[128,128]{1,0:T(8,128)} %param.14) | copy-start | bytes 196612
  6.5 73.5 %all-gather.7.cloned.1.call-start = ((), (), s32[]{:S(2)}) async-start(), calls=%async_computation | async-start | bytes 1114112 | tf_op jit(solution)/shard_map/all_gather | solution.py:31
  10.2 10.6 %collective-permute-start.1 = (f32[2,16,128]{2,1,0:T(8,128)S(1)}, f32[2,16,128]{2,1,0:T(8,128)S(1)}, u32[]{:S(2)}, u32[]{:S(2)}) collective-permute-start(f32[2,16,128]{2,1,0:T(8,128)S(1)} %get-tuple-element.229), channel_id=1, source_target_pairs={{0,1},{1,2},{2,3},{3,4},{4,5},{5,6},{6,7},{7,8},{8,9},{9,10},{10,1... | collective-permute-start | bytes 49160 | tf_op jit(solution)/shard_map/ppermute | solution.py:15
  13.2 7.6 %collective-permute-start.2 = (f32[2,16,128]{2,1,0:T(8,128)S(1)}, f32[2,16,128]{2,1,0:T(8,128)S(1)}, u32[]{:S(2)}, u32[]{:S(2)}) collective-permute-start(f32[2,16,128]{2,1,0:T(8,128)S(1)} %get-tuple-element.230), channel_id=1, source_target_pairs={{1,0},{2,1},{3,2},{4,3},{5,4},{6,5},{7,6},{8,7},{9,8},{10,9},{11,1... | collective-permute-start | bytes 49160 | tf_op jit(solution)/shard_map/ppermute | solution.py:18
  17.1 10.9 %collective-permute-start = (f32[256,128]{1,0:T(8,128)S(1)}, f32[256,128]{1,0:T(8,128)S(1)}, u32[]{:S(2)}, u32[]{:S(2)}) collective-permute-start(f32[256,128]{1,0:T(8,128)S(1)} %get-tuple-element.221), channel_id=1, source_target_pairs={{0,32},{32,64},{64,96},{96,128},{128,160},{160,192},{192,224},{224... | collective-permute-start | bytes 393224 | tf_op jit(solution)/shard_map/ppermute | solution.py:26
  20.1 123.1 %all-gather.9.cloned.1.call-start = ((), (), s32[]{:S(2)}) async-start(), calls=%async_computation.1 | async-start | bytes 2228224 | tf_op jit(solution)/shard_map/all_gather | solution.py:31
  23.4 3.1 %copy-start.2 = (f32[4,128,128]{2,1,0:T(8,128)S(1)}, f32[4,128,128]{2,1,0:T(8,128)}, u32[]{:S(2)}) copy-start(f32[4,128,128]{2,1,0:T(8,128)} %param.16) | copy-start | bytes 786436
  26.1 1.9 copy-start.1
  30.0 9.0 %collective-permute-start.4 = (f32[2,16,128]{2,1,0:T(8,128)S(1)}, f32[2,16,128]{2,1,0:T(8,128)S(1)}, u32[]{:S(2)}, u32[]{:S(2)}) collective-permute-start(f32[2,16,128]{2,1,0:T(8,128)S(1)} %get-tuple-element.227), channel_id=1, source_target_pairs={{0,1},{1,2},{2,3},{3,4},{4,5},{5,6},{6,7},{7,8},{8,9},{9,10},{10,1... | collective-permute-start | bytes 49160 | tf_op jit(solution)/shard_map/ppermute | solution.py:15
  30.0 9.0 %collective-permute-start.5 = (f32[2,16,128]{2,1,0:T(8,128)S(1)}, f32[2,16,128]{2,1,0:T(8,128)S(1)}, u32[]{:S(2)}, u32[]{:S(2)}) collective-permute-start(f32[2,16,128]{2,1,0:T(8,128)S(1)} %get-tuple-element.228), channel_id=1, source_target_pairs={{1,0},{2,1},{3,2},{4,3},{5,4},{6,5},{7,6},{8,7},{9,8},{10,9},{11,1... | collective-permute-start | bytes 49160 | tf_op jit(solution)/shard_map/ppermute | solution.py:18
  35.7 10.5 %collective-permute-start.3 = (f32[256,128]{1,0:T(8,128)S(1)}, f32[256,128]{1,0:T(8,128)S(1)}, u32[]{:S(2)}, u32[]{:S(2)}) collective-permute-start(f32[256,128]{1,0:T(8,128)S(1)} %get-tuple-element.219), channel_id=1, source_target_pairs={{0,32},{32,64},{64,96},{96,128},{128,160},{160,192},{192,224},{224... | collective-permute-start | bytes 393224 | tf_op jit(solution)/shard_map/ppermute | solution.py:26
  178.9 5.7 %collective-permute-start.7 = (f32[2,16,128]{2,1,0:T(8,128)S(1)}, f32[2,16,128]{2,1,0:T(8,128)S(1)}, u32[]{:S(2)}, u32[]{:S(2)}) collective-permute-start(f32[2,16,128]{2,1,0:T(8,128)S(1)} %get-tuple-element.225), channel_id=1, source_target_pairs={{0,1},{1,2},{2,3},{3,4},{4,5},{5,6},{6,7},{7,8},{8,9},{9,10},{10,1... | collective-permute-start | bytes 49160 | tf_op jit(solution)/shard_map/ppermute | solution.py:15
  181.6 3.2 %collective-permute-start.8 = (f32[2,16,128]{2,1,0:T(8,128)S(1)}, f32[2,16,128]{2,1,0:T(8,128)S(1)}, u32[]{:S(2)}, u32[]{:S(2)}) collective-permute-start(f32[2,16,128]{2,1,0:T(8,128)S(1)} %get-tuple-element.226), channel_id=1, source_target_pairs={{1,0},{2,1},{3,2},{4,3},{5,4},{6,5},{7,6},{8,7},{9,8},{10,9},{11,1... | collective-permute-start | bytes 49160 | tf_op jit(solution)/shard_map/ppermute | solution.py:18
  181.6 10.3 %collective-permute-start.6 = (f32[256,128]{1,0:T(8,128)S(1)}, f32[256,128]{1,0:T(8,128)S(1)}, u32[]{:S(2)}, u32[]{:S(2)}) collective-permute-start(f32[256,128]{1,0:T(8,128)S(1)} %get-tuple-element.217), channel_id=1, source_target_pairs={{0,32},{32,64},{64,96},{96,128},{128,160},{160,192},{192,224},{224... | collective-permute-start | bytes 393224 | tf_op jit(solution)/shard_map/ppermute | solution.py:26
  193.9 4.6 %collective-permute-start.10 = (f32[2,16,128]{2,1,0:T(8,128)S(1)}, f32[2,16,128]{2,1,0:T(8,128)S(1)}, u32[]{:S(2)}, u32[]{:S(2)}) collective-permute-start(f32[2,16,128]{2,1,0:T(8,128)S(1)} %get-tuple-element.223), channel_id=1, source_target_pairs={{0,1},{1,2},{2,3},{3,4},{4,5},{5,6},{6,7},{7,8},{8,9},{9,10},{10,1... | collective-permute-start | bytes 49160 | tf_op jit(solution)/shard_map/ppermute | solution.py:15
  195.8 3.5 %collective-permute-start.11 = (f32[2,16,128]{2,1,0:T(8,128)S(1)}, f32[2,16,128]{2,1,0:T(8,128)S(1)}, u32[]{:S(2)}, u32[]{:S(2)}) collective-permute-start(f32[2,16,128]{2,1,0:T(8,128)S(1)} %get-tuple-element.224), channel_id=1, source_target_pairs={{1,0},{2,1},{3,2},{4,3},{5,4},{6,5},{7,6},{8,7},{9,8},{10,9},{11,1... | collective-permute-start | bytes 49160 | tf_op jit(solution)/shard_map/ppermute | solution.py:18
  195.9 10.5 %collective-permute-start.9 = (f32[256,128]{1,0:T(8,128)S(1)}, f32[256,128]{1,0:T(8,128)S(1)}, u32[]{:S(2)}, u32[]{:S(2)}) collective-permute-start(f32[256,128]{1,0:T(8,128)S(1)} %get-tuple-element.215), channel_id=1, source_target_pairs={{0,32},{32,64},{64,96},{96,128},{128,160},{160,192},{192,224},{224... | collective-permute-start | bytes 393224 | tf_op jit(solution)/shard_map/ppermute | solution.py:26
Sparse Core Ops, SparseCore 0:
  20.3 59.7 all-gather.6
  83.1 60.1 all-gather.8
where the time goes:
time: 217 us; the launch traced here: 215 us
  waiting for transfers between devices  78.6 us (36%)
  local copies, waits for them, and re-layouts  35.8 us (16%)
  matrix products  32.4 us (15%)
  starting transfers between devices  27.5 us (13%)
  blocking collectives  18.1 us (8%)
  between operations  14.4 us (7%)
  other arithmetic  6.99 us (3%)
    all_gather x2, waiting for transfers between devices, entering(): pieces = jax.tree.map(lambda part: lax.all_gather(part, axis), value)  77.6 us
    dot_general x47, matrix products, product(): jnp.dot(left, right, precision=lax.Precision.HIGHEST, preferred_element_t...  32.4 us
    all_gather x1, blocking collectives, entering(): pieces = jax.tree.map(lambda part: lax.all_gather(part, axis), value)  18.1 us
    gather x16, local copies, waits for them, and re-layouts, operate(): picked = jnp.take(extended, neighbours[:, face_index], axis=1)  15.6 us
    dynamic_slice x45, local copies, waits for them, and re-layouts, turn(): longer = join(running, jax.tree.map(lambda part: part[position], pieces))  15.4 us
    ppermute x4, starting transfers between devices, passed_along(): return lax.ppermute(x, axis, pairs)  10.1 us
    ppermute x4, starting transfers between devices, with_halo(): lax.ppermute(lax.slice_in_dim(block, 0, width, axis=dim), axis, backward)  9.63 us
    ppermute x4, starting transfers between devices, with_halo(): lax.ppermute(lax.slice_in_dim(block, block.shape[dim] - width, None, axis...  7.68 us
  transfers between devices with their start and end apart: 14, of which 4 were waited for; matrix products, arithmetic and copies ran while one was open for 16% of the time, Pallas kernels for 0%

commit v1 on v0

v1 whole, which is shorter than its diff:
```python
import jax
import jax.numpy as jnp
from jax import lax
from jax.experimental import pallas as pl
from jax.experimental.pallas import tpu as pltpu
from jax.sharding import PartitionSpec as P

DAMPING = 0.7
F32 = jnp.float32
BF16 = jnp.bfloat16
MESH = pl.DeviceIdType.MESH


def dot(left, right):
    return jnp.dot(left, right, preferred_element_type=F32)


def split(x):
    high = x.astype(BF16)
    low = (x - high.astype(F32)).astype(BF16)
    return jnp.concatenate([high, low], axis=1)


def halves(x):
    width = x.shape[1] // 2
    return x[:, :width] + x[:, width:]


def weights(matrix):
    parts = split(matrix)
    return jnp.concatenate([parts, parts], axis=0)


def iota(shape, dim):
    return lax.broadcasted_iota(jnp.int32, shape, dim)


def column(row):
    size = row.shape[1]
    same = iota((size, size), 0) == iota((size, size), 1)
    return jnp.sum(jnp.where(same, row, 0.0), axis=1, keepdims=True)


def later(blocks, by):
    zeros = jnp.zeros((16 * by, blocks.shape[1]), F32)
    return jnp.concatenate([zeros, blocks[: -16 * by]], axis=0)


def kernel(
    groups, partitions,
    source_hbm, scale_hbm, inverse_hbm, flux_hbm, trace_hbm, neighbours_hbm, send_hbm,
    out_ref,
    source, scale_row, inverse, flux, trace, neighbours, send_row,
    pick, halo_pick, face_w, time_w, near_w, far_w, gathered,
    v0_last, v0_sent, v1_sent, c_sent, v3_sent, v3_last,
    halo0, halo1, halo_c, halo3, before0, before_sent, before3,
    rhs, rhs_all, chain_out, chain_all, scale_full,
    in_sem, send_sem, recv_sem,
):
    k = lax.axis_index("tm")
    p = lax.axis_index("space")
    loads = [
        pltpu.make_async_copy(src, dst, in_sem.at[i])
        for i, (src, dst) in enumerate(
            [
                (scale_hbm, scale_row), (send_hbm, send_row), (source_hbm, source), (inverse_hbm, inverse),
                (neighbours_hbm, neighbours), (flux_hbm, flux), (trace_hbm, trace),
            ]
        )
    ]
    for load in loads:
        load.start()
    left = {"space": lax.rem(p + partitions - 1, partitions)}
    right = {"space": lax.rem(p + 1, partitions)}
    others = [lax.rem(k + d, groups) for d in range(1, groups)]
    after = {"tm": others[0]}

    barrier = pltpu.get_barrier_semaphore()
    for partner in [left, right] + [{"tm": other} for other in others]:
        pl.semaphore_signal(barrier, inc=1, device_id=partner, device_id_type=MESH)

    def remote(src, dst, number, device):
        return pltpu.make_async_remote_copy(
            src_ref=src, dst_ref=dst, send_sem=send_sem.at[number], recv_sem=recv_sem.at[number],
            device_id=device, device_id_type=MESH,
        )

    def halo_copies(sent, received, number):
        if len(sent.shape) == 3:
            return [
                remote(sent.at[:, 16:32], received.at[:, 0:16], number, right),
                remote(sent.at[:, 0:16], received.at[:, 16:32], number + 1, left),
            ]
        return [
            remote(sent.at[16:32], received.at[0:16], number, right),
            remote(sent.at[0:16], received.at[16:32], number + 1, left),
        ]

    for load in loads[:4]:
        load.wait()
    scale = column(scale_row[...])
    scale_full[...] = jnp.broadcast_to(scale, (256, 128))
    sigma = DAMPING / scale
    coarse = 1.0 / (2.0 * scale - 1.0)
    send_col = column(send_row[...].astype(F32))
    choose = iota((32, 256), 1).astype(F32) == send_col
    sent_sigma = DAMPING / jnp.sum(jnp.where(choose, scale_row[...], 0.0), axis=1, keepdims=True)
    choose = jnp.where(choose, 1.0, 0.0).astype(BF16)
    inverse_w = weights(inverse[...])
    a0 = halves(dot(split(source[0]), inverse_w))
    a1 = halves(dot(split(source[1]), inverse_w))
    v0_0 = sigma * a0
    v0_1 = sigma * a1
    v0_last[...] = v0_1
    s0 = split(v0_0)
    s1 = split(v0_1)
    v0_sent[0] = halves(dot(choose, s0))
    v0_sent[1] = halves(dot(choose, s1))
    pl.semaphore_wait(barrier, groups + 1)

    first_halo = halo_copies(v0_sent, halo0, 0)
    first_sent = remote(v0_sent.at[1], before_sent, 2, after)
    first_last = remote(v0_last, before0, 3, after)
    for copy in first_halo + [first_sent, first_last]:
        copy.start()

    for load in loads[4:]:
        load.wait()
    flux_b = halves(dot(split(flux[...].reshape(512, 128)), inverse_w))
    for f in range(4):
        face_w[f * 256 : (f + 1) * 256, :] = weights(flux_b[f * 128 : (f + 1) * 128])
    m1 = halves(dot(split(trace[...]), inverse_w))
    w1 = weights(m1)
    time_w[...] = w1
    lanes = iota((256, 256), 1).astype(F32)
    lane = iota((256, 128), 1)
    halo_hit = jnp.zeros((256, 128), F32)
    for f in range(4):
        names = column(neighbours[f : f + 1, :].astype(F32))
        pick[f * 256 : (f + 1) * 256, :] = jnp.where(lanes == names, 1.0, 0.0).astype(BF16)
        target = jnp.where(lane // 32 == f, lane % 32 + 256, -1).astype(F32)
        halo_hit = halo_hit + jnp.where(target == names, 1.0, 0.0)
    halo_hit = halo_hit.astype(BF16)
    halo_pick[...] = halo_hit
    halo_sent = dot(choose, halo_hit).astype(BF16)

    def faces(parts):
        for f in range(4):
            rows = dot(pick[f * 256 : (f + 1) * 256, :], parts)
            gathered[:, f * 256 : (f + 1) * 256] = rows.astype(BF16)
        return halves(dot(gathered[...], face_w[...]))

    def timed(parts):
        return halves(dot(parts, time_w[...]))

    def halo_parts(rows):
        parts = split(rows)
        each = [halves(dot(parts, face_w[f * 256 : (f + 1) * 256, :])) for f in range(4)]
        return split(jnp.concatenate(each, axis=0))

    def chosen(x):
        return halves(dot(choose, split(x)))

    base1 = 1.3 * v0_1 + sigma * (faces(s1) + timed(s0))
    base0 = 1.3 * v0_0 + sigma * faces(s0)
    sent_base1 = chosen(base1)
    sent_base0 = chosen(base0)
    for copy in first_halo + [first_sent]:
        copy.wait()
    started = k > 0
    h0 = halo_parts(halo0[0])
    h1 = halo_parts(halo0[1])
    early = jnp.where(started, before_sent[...], 0.0)
    v1_sent[0] = sent_base0 + sent_sigma * (halves(dot(halo_sent, h0)) + timed(split(early)))
    v1_sent[1] = sent_base1 + sent_sigma * halves(dot(halo_sent, h1))
    second_halo = halo_copies(v1_sent, halo1, 4)
    for copy in second_halo:
        copy.start()
    v1_1 = base1 + sigma * halves(dot(halo_pick[...], h1))
    base0 = base0 + sigma * halves(dot(halo_pick[...], h0))
    r1 = a1 - scale * v1_1 + faces(split(v1_1))
    first_last.wait()
    v1_0 = base0 + sigma * timed(split(jnp.where(started, before0[...], 0.0)))
    s0 = split(v1_0)
    r1 = r1 + timed(s0)
    total = r1 + a0 - scale * v1_0 + faces(s0)
    for copy in second_halo:
        copy.wait()
    h1 = halo1[1]
    both = halo_parts(halo1[0] + h1)
    total = total + halves(dot(halo_pick[...], both))
    rhs[...] = coarse * total + v1_1
    mine = pl.ds(pl.multiple_of(k * 16, 16), 16)

    def exchange(src, dst, number):
        for other in others:
            theirs = pl.ds(pl.multiple_of(other * 16, 16), 16)
            remote(src.at[theirs], dst.at[mine], number, {"tm": other}).start()
        count = pl.ds(0, 16 * (groups - 1))
        return remote(src.at[count], dst.at[count], number, after)

    to_owners = exchange(rhs, rhs_all, 6)
    rhs_all[mine, :] = rhs[mine, :]
    r1 = r1 + halves(dot(halo_pick[...], halo_parts(h1)))
    step = r1 * sigma
    pre0 = v1_0 - step
    pre1 = step

    m2 = halves(dot(split(m1), w1))
    w2 = weights(m2)
    m34 = halves(dot(split(jnp.concatenate([m1, m2], axis=0)), w2))
    m3, m4 = m34[:128], m34[128:]
    w4 = weights(m4)
    m8 = halves(dot(split(m4), w4))
    m12 = halves(dot(split(m8), w4))
    for i, w in enumerate([w1, w2, weights(m3)]):
        near_w[:, i * 256 : (i + 1) * 256] = w
    for i, w in enumerate([w4, weights(m8), weights(m12)]):
        far_w[:, i * 256 : (i + 1) * 256] = w
    own_scale = scale_full[mine, :]
    own_scale = 1.0 / (2.0 * own_scale - 1.0)
    c1 = jnp.concatenate([own_scale] * groups, axis=0)
    c2 = c1 * c1
    c4 = c2 * c2
    c8 = c4 * c4

    to_owners.wait()
    x = rhs_all[...]
    y = dot(split(x), near_w[...])
    x = (
        x
        + later(c1 * halves(y[:, 0:256]), 1)
        + later(c2 * halves(y[:, 256:512]), 2)
        + later(c1 * c2 * halves(y[:, 512:768]), 3)
    )
    y = dot(split(x), far_w[...])
    x = (
        x
        + later(c4 * halves(y[:, 0:256]), 4)
        + later(c8 * halves(y[:, 256:512]), 8)
        + later(c4 * c8 * halves(y[:, 512:768]), 12)
    )
    chain_out[...] = x
    to_slabs = exchange(chain_out, chain_all, 7)
    chain_all[mine, :] = chain_out[mine, :]
    to_slabs.wait()

    w = chain_all[...]
    c = w - v1_1
    sc = split(c)
    c_sent[...] = halves(dot(choose, sc))
    third_halo = halo_copies(c_sent, halo_c, 8)
    for copy in third_halo:
        copy.start()
    fc = faces(sc)
    base0 = pre0 + (1.0 + DAMPING - sigma) * c + sigma * fc
    base1 = w + pre1 - DAMPING * c + sigma * (fc + timed(sc))
    sent_base0 = chosen(base0)
    sent_base1 = chosen(base1)
    for copy in third_halo:
        copy.wait()
    hc = halo_parts(halo_c[...])
    extra = sent_sigma * halves(dot(halo_sent, hc))
    v3_sent[0] = sent_base0 + extra
    v3_sent[1] = sent_base1 + extra
    fourth_halo = halo_copies(v3_sent, halo3, 10)
    for copy in fourth_halo:
        copy.start()
    extra = sigma * halves(dot(halo_pick[...], hc))
    v3_1 = base1 + extra
    v3_last[...] = v3_1
    last = remote(v3_last, before3, 12, after)
    last.start()
    v3_0 = base0 + extra
    s0 = split(v3_0)
    s1 = split(v3_1)
    u1 = faces(s1) + timed(s0)
    u0 = faces(s0)
    for copy in fourth_halo:
        copy.wait()
    u1 = u1 + halves(dot(halo_pick[...], halo_parts(halo3[1])))
    out_ref[1] = v0_last[...] + (1.0 - DAMPING) * v3_1 + sigma * u1
    u0 = u0 + halves(dot(halo_pick[...], halo_parts(halo3[0])))
    base0 = sigma * a0 + (1.0 - DAMPING) * v3_0 + sigma * u0
    last.wait()
    out_ref[0] = base0 + sigma * timed(split(jnp.where(started, before3[...], 0.0)))


def solution(mesh):
    groups, partitions = mesh.shape["tm"], mesh.shape["space"]

    def body(source, elem_scale, diag_block, block_inverse, face_flux, time_trace, neighbours, send_rows):
        any_space = pl.BlockSpec(memory_space=pl.ANY)
        vmem = pltpu.VMEM
        rows = (256, 128)
        return pl.pallas_call(
            lambda *refs: kernel(groups, partitions, *refs),
            out_shape=jax.ShapeDtypeStruct((2, 256, 128), F32),
            in_specs=[any_space] * 7,
            out_specs=pl.BlockSpec(memory_space=pltpu.VMEM),
            scratch_shapes=[
                vmem((2, 256, 128), F32), vmem((1, 256), F32), vmem((128, 128), F32), vmem((4, 128, 128), F32),
                vmem((128, 128), F32), vmem((4, 256), jnp.int32), vmem((1, 32), jnp.int32),
                vmem((1024, 256), BF16), vmem((256, 128), BF16), vmem((1024, 256), BF16), vmem((256, 256), BF16),
                vmem((256, 768), BF16), vmem((256, 768), BF16), vmem((256, 1024), BF16),
                vmem(rows, F32), vmem((2, 32, 128), F32), vmem((2, 32, 128), F32), vmem((32, 128), F32),
                vmem((2, 32, 128), F32), vmem(rows, F32),
                vmem((2, 32, 128), F32), vmem((2, 32, 128), F32), vmem((32, 128), F32), vmem((2, 32, 128), F32),
                vmem(rows, F32), vmem((32, 128), F32), vmem(rows, F32),
                vmem(rows, F32), vmem(rows, F32), vmem(rows, F32), vmem(rows, F32), vmem(rows, F32),
                pltpu.SemaphoreType.DMA((7,)), pltpu.SemaphoreType.DMA((13,)), pltpu.SemaphoreType.DMA((13,)),
            ],
            compiler_params=pltpu.CompilerParams(
                collective_id=0, has_side_effects=True, vmem_limit_bytes=32 * 1024 * 1024
            ),
        )(source, elem_scale.reshape(1, 256), block_inverse, face_flux, time_trace, neighbours.T, send_rows)

    return jax.shard_map(
        body,
        mesh=mesh,
        in_specs=(P("tm", "space", None), P("space"), P(), P(), P(), P(), P("space", None), P("space", None)),
        out_specs=P("tm", "space", None),
        check_vma=False,
    )
```

time: 217 us -> 46 us (0.21)
  waiting for transfers between devices: 78.6 us -> 0 us
  Pallas kernels: 0 us -> 40 us
  matrix products: 32.4 us -> 0 us
  local copies, waits for them, and re-layouts: 35.8 us -> 5.65 us
  starting transfers between devices: 27.5 us -> 0 us
  blocking collectives: 18.1 us -> 0 us
  between operations: 14.4 us -> 0.02 us
  other arithmetic: 6.99 us -> 0 us
    all_gather x2 -> x0, waiting for transfers between devices: 77.6 us -> none  [entering(): pieces = jax.tree.map(lambda part: lax.all_gather(part, axis), value)]
    pallas_call x0 -> x1, Pallas kernels: none -> 40 us  [body(): pl.pallas_call(lambda *refs: kernel(groups, partitions, *refs), out_shape...]
    dot_general x47 -> x0, matrix products: 32.4 us -> none  [product(): jnp.dot(left, right, precision=lax.Precision.HIGHEST, preferred_element_t...]
    ppermute x12 -> x0, starting transfers between devices: 27.5 us -> none  [the longest x4 10.1 us: passed_along(): return lax.ppermute(x, axis, pairs)]
    all_gather x1 -> x0, blocking collectives: 18.1 us -> none  [entering(): pieces = jax.tree.map(lambda part: lax.all_gather(part, axis), value)]
    gather x24 -> x0, local copies, waits for them, and re-layouts: 18.1 us -> none  [the longest x16 15.6 us: operate(): picked = jnp.take(extended, neighbours[:, face_index], axis=1)]
    dynamic_slice x45 -> x0, local copies, waits for them, and re-layouts: 15.4 us -> none  [turn(): longer = join(running, jax.tree.map(lambda part: part[position], pieces))]
    select_n x21 -> x0, other arithmetic: 6.06 us -> none  [the longest x20 5.4 us: operate(): picked = jnp.take(extended, neighbours[:, face_index], axis=1)]
  transfers between devices with their start and end apart: 14 -> 0, of which waited for: 4 -> 0; matrix products, arithmetic and copies ran while one was open for 16% -> 0% of each run, Pallas kernels for 0% -> 0%
where the time goes in v1:
time: 46 us; the launch traced here: 45.7 us
  Pallas kernels  40 us (87%)
  local copies, waits for them, and re-layouts  5.65 us (12%)
    pallas_call x1, Pallas kernels, body(): pl.pallas_call(lambda *refs: kernel(groups, partitions, *refs), out_shape...  40 us
    unnamed x15, local copies, waits for them, and re-layouts  5.65 us

profile of v1, /device:TPU:1, one launch (start us, length us, event | category | flops | bytes accessed | tf_op | source)
XLA Modules:
  0.0 45.7 jit_solution(11466906439640705985)
XLA Ops:
  0.0 0.0 copy-start.5
  0.0 0.0 copy-start.6
  0.0 0.7 %copy-done.5 = f32[256]{0:T(256)S(1)} copy-done((f32[256]{0:T(256)S(1)}, f32[256]{0:T(256)}, u32[]{:S(2)}) %copy-start.5) | copy-done | bytes 1048
  0.7 0.0 copy-done.6
  0.7 0.0 copy-start
  0.7 0.9 %copy-done = f32[2,256,128]{2,1,0:T(8,128)S(1)} copy-done((f32[2,256,128]{2,1,0:T(8,128)S(1)}, f32[2,256,128]{2,1,0:T(8,128)}, u32[]{:S(2)}) %copy-start) | copy-done | bytes 262168
  1.6 0.0 copy-start.1
  1.6 0.9 %copy-done.1 = f32[4,128,128]{2,1,0:T(8,128)S(1)} copy-done((f32[4,128,128]{2,1,0:T(8,128)S(1)}, f32[4,128,128]{2,1,0:T(8,128)}, u32[]{:S(2)}) %copy-start.1) | copy-done | bytes 262168
  2.6 0.0 copy-start.2
  2.6 0.8 %copy-done.2 = f32[128,128]{1,0:T(8,128)S(1)} copy-done((f32[128,128]{1,0:T(8,128)S(1)}, f32[128,128]{1,0:T(8,128)}, u32[]{:S(2)}) %copy-start.2) | copy-done | bytes 65560
  3.4 0.0 copy-start.3
  3.4 0.8 %copy-done.3 = f32[128,128]{1,0:T(8,128)S(1)} copy-done((f32[128,128]{1,0:T(8,128)S(1)}, f32[128,128]{1,0:T(8,128)}, u32[]{:S(2)}) %copy-start.3) | copy-done | bytes 65560
  4.3 0.0 copy-start.4
  4.3 0.7 %copy-done.4 = s32[256,4]{0,1:T(4,128)S(1)} copy-done((s32[256,4]{0,1:T(4,128)S(1)}, s32[256,4]{0,1:T(4,128)}, u32[]{:S(2)}) %copy-start.4) | copy-done | bytes 4120
  5.0 40.0 %shard_map.73 = f32[2,256,128]{2,1,0:T(8,128)S(1)} custom-call(f32[2,256,128]{2,1,0:T(8,128)S(1)} %copy-done, f32[1,256]{1,0:T(1,128)S(1)} %bitcast.3, f32[128,128]{1,0:T(8,128)S(1)} %copy-done.2, f32[4,128,128]{2,1,0:T(8,128)S(1)} %copy-done.1, f32[128,128]{1,0:T(8,128)S(1)} %copy-done.3, s32[4,256]{1,0:T(4,128)S(1)} %bitcast.2, s32[1,32]{1,0:T(1,128)S(1)} %copy-done.6), custom_call_target="tpu_custom_call" | custom-call | tf_op jit(solution)/shard_map/pallas_call | solution.py:296
  45.0 0.7 %copy.9 = f32[2,256,128]{2,1,0:T(8,128)} copy(f32[2,256,128]{2,1,0:T(8,128)S(1)} %shard_map.73) | data formatting | bytes 524288
Async XLA Ops:
  0.0 0.7 %copy-start.5 = (f32[256]{0:T(256)S(1)}, f32[256]{0:T(256)}, u32[]{:S(2)}) copy-start(f32[256]{0:T(256)} %param.9) | copy-start | bytes 3076
  0.0 0.7 %copy-start.6 = (s32[1,32]{1,0:T(1,128)S(1)}, s32[1,32]{1,0:T(1,128)}, u32[]{:S(2)}) copy-start(s32[1,32]{1,0:T(1,128)} %refs_6_.1) | copy-start | bytes 388
  0.7 1.0 %copy-start = (f32[2,256,128]{2,1,0:T(8,128)S(1)}, f32[2,256,128]{2,1,0:T(8,128)}, u32[]{:S(2)}) copy-start(f32[2,256,128]{2,1,0:T(8,128)} %refs_0_.1) | copy-start | bytes 786436
  1.6 0.9 %copy-start.1 = (f32[4,128,128]{2,1,0:T(8,128)S(1)}, f32[4,128,128]{2,1,0:T(8,128)}, u32[]{:S(2)}) copy-start(f32[4,128,128]{2,1,0:T(8,128)} %refs_3_.1) | copy-start | bytes 786436
  2.6 0.8 %copy-start.2 = (f32[128,128]{1,0:T(8,128)S(1)}, f32[128,128]{1,0:T(8,128)}, u32[]{:S(2)}) copy-start(f32[128,128]{1,0:T(8,128)} %refs_2_.1) | copy-start | bytes 196612
  3.4 0.8 %copy-start.3 = (f32[128,128]{1,0:T(8,128)S(1)}, f32[128,128]{1,0:T(8,128)}, u32[]{:S(2)}) copy-start(f32[128,128]{1,0:T(8,128)} %refs_4_.1) | copy-start | bytes 196612
  4.3 0.7 %copy-start.4 = (s32[256,4]{0,1:T(4,128)S(1)}, s32[256,4]{0,1:T(4,128)}, u32[]{:S(2)}) copy-start(s32[256,4]{0,1:T(4,128)} %param.13) | copy-start | bytes 12292

commit v2 on v1

v2 whole, which is shorter than its diff:
```python
import jax
import jax.numpy as jnp
from jax import lax
from jax.experimental import pallas as pl
from jax.experimental.pallas import tpu as pltpu
from jax.sharding import PartitionSpec as P

DAMPING = 0.7
KEEP = 1.0 - DAMPING
F32 = jnp.float32
BF16 = jnp.bfloat16
MESH = pl.DeviceIdType.MESH


def dot(left, right):
    return jnp.dot(left, right, preferred_element_type=F32)


def split(x):
    high = x.astype(BF16)
    low = (x - high.astype(F32)).astype(BF16)
    return jnp.concatenate([high, low], axis=1)


def halves(x):
    width = x.shape[1] // 2
    return x[:, :width] + x[:, width:]


def weights(matrix):
    parts = split(matrix)
    return jnp.concatenate([parts, parts], axis=0)


def iota(shape, dim):
    return lax.broadcasted_iota(jnp.int32, shape, dim)


def column(row):
    size = row.shape[1]
    same = iota((size, size), 0) == iota((size, size), 1)
    return jnp.sum(jnp.where(same, row, 0.0), axis=1, keepdims=True)


def onehot(hit):
    return jnp.where(hit, 1.0, 0.0).astype(BF16)


def any_hit(hits):
    total = jnp.where(hits[0], 1.0, 0.0)
    for hit in hits[1:]:
        total = total + jnp.where(hit, 1.0, 0.0)
    return total.astype(BF16)


def later(blocks, by):
    zeros = jnp.zeros((16 * by, blocks.shape[1]), F32)
    return jnp.concatenate([zeros, blocks[: -16 * by]], axis=0)


def kernel(
    groups, partitions,
    source_hbm, scale_hbm, inverse_hbm, flux_hbm, trace_hbm, neighbours_hbm, send_hbm,
    out_ref,
    source, scale_row, inverse, flux, trace, neighbours, send_row,
    pick, spread, face_w, near_w, far_w, gathered,
    v0_last, out1, in1, far1, diag1, before0,
    rhs, rhs_all, carry, before_carry, chain_out, chain_all, out3, in3, far3, scale_full,
    in_sem, send_sem, recv_sem,
):
    k = lax.axis_index("tm")
    p = lax.axis_index("space")
    loads = [
        pltpu.make_async_copy(src, dst, in_sem.at[i])
        for i, (src, dst) in enumerate(
            [
                (scale_hbm, scale_row), (send_hbm, send_row), (neighbours_hbm, neighbours), (inverse_hbm, inverse),
                (source_hbm, source), (flux_hbm, flux), (trace_hbm, trace),
            ]
        )
    ]
    for load in loads:
        load.start()

    def space(by):
        return lax.rem(p + partitions + by, partitions)

    others = []
    for hops in (4, 3, 2, 1):
        for dy in range(4):
            for dx in range(4):
                if min(dy, 4 - dy) + min(dx, 4 - dx) == hops:
                    others.append(lax.rem(k // 4 + dy, 4) * 4 + lax.rem(lax.rem(k, 4) + dx, 4))
    after = lax.rem(k + 1, groups)
    ahead = lax.rem(k + groups - 1, groups)

    barrier = pltpu.get_barrier_semaphore()
    senders = [{"tm": other} for other in others]
    senders += [{"space": space(by)} for by in (1, -1, 2, -2)]
    senders += [{"tm": ahead, "space": space(by)} for by in (1, -1)]
    for partner in senders:
        pl.semaphore_signal(barrier, inc=1, device_id=partner, device_id_type=MESH)

    def remote(src, dst, number, device):
        return pltpu.make_async_remote_copy(
            src_ref=src, dst_ref=dst, send_sem=send_sem.at[number], recv_sem=recv_sem.at[number],
            device_id=device, device_id_type=MESH,
        )

    for load in loads[:3]:
        load.wait()
    scale = column(scale_row[...])
    scale_full[...] = jnp.broadcast_to(scale, (256, 128))
    sigma = DAMPING / scale
    coarse = 1.0 / (2.0 * scale - 1.0)
    send_f = send_row[...].astype(F32)
    send_col = column(send_f)
    lanes = iota((256, 256), 1).astype(F32)
    choose_hit = iota((32, 256), 1).astype(F32) == send_col
    choose = onehot(choose_hit)
    sent_scale = jnp.sum(jnp.where(choose_hit, scale_row[...], 0.0), axis=1, keepdims=True)
    sent_sigma = DAMPING / sent_scale
    name_rows = [neighbours[f : f + 1, :].astype(F32) for f in range(4)]
    sent_names = [jnp.sum(jnp.where(choose_hit, row, 0.0), axis=1, keepdims=True) for row in name_rows]
    wide = iota((32, 256), 1).astype(F32)
    sent_pick = jnp.concatenate([onehot(wide == names) for names in sent_names], axis=0)

    def halo_hits(names, size):
        lane = iota((size, 128), 1)
        hits = []
        for f in range(4):
            target = jnp.where(lane // 32 == f, lane % 32 + 256, -1).astype(F32)
            hits.append(target == names[f])
        return any_hit(hits)

    halo_sent = halo_hits(sent_names, 32)
    lane = iota((32, 128), 1)
    facts = jnp.where(lane == 4, sent_sigma, 0.0)
    for f in range(4):
        facts = facts + jnp.where(lane == f, sent_names[f], 0.0)
    out1[4] = facts

    loads[3].wait()
    inverse_w = weights(inverse[...])
    loads[4].wait()
    v0_0 = sigma * halves(dot(split(source[0]), inverse_w))
    v0_1 = sigma * halves(dot(split(source[1]), inverse_w))
    v0_last[...] = v0_1
    a0 = v0_0 * scale * (1.0 / DAMPING)
    a1 = v0_1 * scale * (1.0 / DAMPING)
    for load in loads[5:]:
        load.wait()
    flux_b = halves(dot(split(flux[...].reshape(512, 128)), inverse_w))
    for f in range(4):
        face_w[f * 256 : (f + 1) * 256, :] = weights(flux_b[f * 128 : (f + 1) * 128])
    m1 = halves(dot(split(trace[...]), inverse_w))
    w1 = weights(m1)
    near_w[:, 0:256] = w1
    s0 = split(v0_0)
    s1 = split(v0_1)
    own0 = halves(dot(choose, s0))
    own1 = halves(dot(choose, s1))
    out1[0] = own0
    out1[1] = own1

    def timed(x):
        return halves(dot(split(x), near_w[:, 0:256]))

    def sent_faces(parts):
        rows = dot(sent_pick, parts).astype(BF16)
        rows = jnp.concatenate([rows[f * 32 : (f + 1) * 32] for f in range(4)], axis=1)
        return halves(dot(rows, face_w[...]))

    out1[2] = (1.0 + KEEP) * own0 + sent_sigma * sent_faces(s0)
    out1[3] = (1.0 + KEEP) * own1 + sent_sigma * (sent_faces(s1) + timed(own0))
    pl.semaphore_wait(barrier, groups + 5)

    to_right, to_left = pl.ds(16, 16), pl.ds(0, 16)
    first = [
        remote(out1.at[:, to_right], in1.at[:, to_left], 0, {"space": space(1)}),
        remote(out1.at[:, to_left], in1.at[:, to_right], 1, {"space": space(-1)}),
        remote(out1.at[0:2, to_right], far1.at[:, to_left], 2, {"space": space(2)}),
        remote(out1.at[0:2, to_left], far1.at[:, to_right], 3, {"space": space(-2)}),
        remote(out1.at[1, to_right], diag1.at[to_left], 4, {"tm": after, "space": space(1)}),
        remote(out1.at[1, to_left], diag1.at[to_right], 5, {"tm": after, "space": space(-1)}),
    ]
    first_last = remote(v0_last, before0, 6, {"tm": after})
    for copy in first + [first_last]:
        copy.start()

    send4 = jnp.concatenate([send_col] * 4, axis=0)
    eye = iota((128, 128), 0) == iota((128, 128), 1)
    send4 = jnp.sum(jnp.where(eye, send4, 0.0), axis=0, keepdims=True)
    names = [column(row) for row in name_rows]
    for f in range(4):
        pick[f * 256 : (f + 1) * 256, :] = onehot(lanes == names[f])
    spread[:, 0:128] = halo_hits(names, 256)
    lane = iota((256, 128), 1)
    spread[:, 128:256] = any_hit([(jnp.where(lane // 32 == f, send4, -1.0) == names[f]) for f in range(4)])
    element = iota((256, 128), 0).astype(F32)
    spread[:, 256:384] = onehot(jnp.where(lane < 32, send4, -1.0) == element)

    def gather(parts, ref):
        for f in range(4):
            rows = dot(pick[f * 256 : (f + 1) * 256, :], parts)
            ref[:, f * 256 : (f + 1) * 256] = rows.astype(BF16)
        return halves(dot(ref[...], face_w[...]))

    def faces(x):
        return gather(split(x), gathered)

    def stacks(rows):
        parts = split(rows)
        each = [halves(dot(parts, face_w[f * 256 : (f + 1) * 256, :])) for f in range(4)]
        count = rows.shape[0] // 32
        return [jnp.concatenate([e[i * 32 : (i + 1) * 32] for e in each], axis=0) for i in range(count)]

    def scattered(halo_stack, change_stack, own_rows):
        rest = jnp.zeros((96, 128), F32)
        right = jnp.concatenate([halo_stack, change_stack, own_rows, rest], axis=0)
        return halves(dot(spread[...], split(right)))

    def chosen(x):
        return halves(dot(choose, split(x)))

    base1 = (1.0 + KEEP) * v0_1 + sigma * (gather(s1, gathered) + timed(v0_0))
    base0 = (1.0 + KEEP) * v0_0 + sigma * gather(s0, gathered)
    rest1 = a1 - scale * base1 + faces(base1) + timed(base0)
    rest0 = a0 - scale * base0 + faces(base0)

    for copy in first:
        copy.wait()
    started = k > 0
    facts = in1[4]
    far_names = [facts[:, f : f + 1] for f in range(4)]
    halo_sigma = facts[:, 4:5]
    far_hits = halo_hits(far_names, 32).astype(F32)
    upper = iota((32, 128), 0) < 16
    far_halo = jnp.concatenate([jnp.where(upper, far_hits, 0.0), jnp.where(upper, 0.0, far_hits)], axis=1).astype(BF16)

    def seen_by_halo(far, own):
        return [far[0:16], own[0:16], own[16:32], far[16:32]]

    st = stacks(
        jnp.concatenate([in1[0], in1[1]] + seen_by_halo(far1[0], own0) + seen_by_halo(far1[1], own1), axis=0)
    )
    change0 = sent_sigma * halves(dot(halo_sent, split(st[0])))
    change1 = sent_sigma * halves(dot(halo_sent, split(st[1])))
    halo_v0 = in1[2] + halo_sigma * (
        halves(dot(far_halo, split(jnp.concatenate(st[2:4], axis=0)))) + timed(jnp.where(started, diag1[...], 0.0))
    )
    halo_v1 = in1[3] + halo_sigma * halves(dot(far_halo, split(jnp.concatenate(st[4:6], axis=0))))
    st = stacks(jnp.concatenate([halo_v0, halo_v1, change0, change1], axis=0))
    rest1 = rest1 + scattered(st[1], st[3], timed(change0) - sent_scale * change1)
    rest0 = rest0 + scattered(st[0], st[2], -sent_scale * change0)
    place = spread[:, 256:384]
    rest = jnp.zeros((96, 128), F32)
    v1_1 = base1 + halves(dot(place, split(jnp.concatenate([change1, rest], axis=0))))
    base0 = base0 + halves(dot(place, split(jnp.concatenate([change0, rest], axis=0))))
    ready = coarse * (rest0 + rest1) + v1_1

    first_last.wait()
    delta = sigma * timed(jnp.where(started, before0[...], 0.0))
    t_delta = timed(delta)
    rhs[...] = ready + coarse * (faces(delta) + t_delta - scale * delta)
    mine = pl.ds(pl.multiple_of(k * 16, 16), 16)

    def block(i, size=16):
        return pl.ds(pl.multiple_of(i * 16, 16), size)

    for other in others:
        remote(rhs.at[block(other)], rhs_all.at[mine], 7, {"tm": other}).start()
    count = pl.ds(0, 16 * (groups - 1))
    to_owners = remote(rhs.at[count], rhs_all.at[count], 7, {"tm": after})
    rhs_all[mine, :] = rhs[mine, :]

    v1_0 = base0 + delta
    step = sigma * (rest1 + t_delta)
    carry[...] = v0_1 + sigma * timed(v1_0 - v1_1)
    carried = remote(carry, before_carry, 8, {"tm": after})
    carried.start()
    pre0 = v1_0 - step
    pre1 = v1_1 + step
    sent_pre0 = chosen(pre0)
    sent_pre1 = chosen(pre1)
    pre1 = step

    m2 = halves(dot(split(m1), w1))
    w2 = weights(m2)
    m34 = halves(dot(split(jnp.concatenate([m1, m2], axis=0)), w2))
    m3, m4 = m34[:128], m34[128:]
    w4 = weights(m4)
    m8 = halves(dot(split(m4), w4))
    m12 = halves(dot(split(m8), w4))
    near_w[:, 256:512] = w2
    near_w[:, 512:768] = weights(m3)
    for i, w in enumerate([w4, weights(m8), weights(m12)]):
        far_w[:, i * 256 : (i + 1) * 256] = w
    own_scale = scale_full[mine, :]
    own_scale = 1.0 / (2.0 * own_scale - 1.0)
    c1 = jnp.concatenate([own_scale] * groups, axis=0)
    c2 = c1 * c1
    c4 = c2 * c2
    c8 = c4 * c4
    chain_out[0:16, :] = jnp.zeros((16, 128), F32)

    to_owners.wait()
    x = rhs_all[...]
    y = dot(split(x), near_w[...])
    x = (
        x
        + later(c1 * halves(y[:, 0:256]), 1)
        + later(c2 * halves(y[:, 256:512]), 2)
        + later(c1 * c2 * halves(y[:, 512:768]), 3)
    )
    y = dot(split(x), far_w[...])
    chain_out[16:272, :] = (
        x
        + later(c4 * halves(y[:, 0:256]), 4)
        + later(c8 * halves(y[:, 256:512]), 8)
        + later(c4 * c8 * halves(y[:, 512:768]), 12)
    )
    for other in others:
        remote(chain_out.at[block(other, 32)], chain_all.at[k], 9, {"tm": other}).start()
    to_slabs = remote(chain_all.at[pl.ds(0, groups - 1)], chain_all.at[pl.ds(0, groups - 1)], 9, {"tm": after})
    chain_all[k] = chain_out[block(k, 32), :]
    for copy in (to_slabs, carried):
        copy.wait()

    w = chain_all[:, 16:32].reshape(256, 128)
    wp = chain_all[:, 0:16].reshape(256, 128)
    c = w - v1_1
    sc = split(c)
    sp = split(wp)
    sent_c = halves(dot(choose, sc))
    sent_fc = sent_faces(sc)
    out3[0] = sent_c
    out3[1] = halves(dot(choose, sp))
    out3[2] = sent_pre0 + (1.0 + DAMPING - sent_sigma) * sent_c + sent_sigma * sent_fc
    out3[3] = sent_pre1 + KEEP * sent_c + sent_sigma * (sent_fc + timed(sent_c))
    second = [
        remote(out3.at[:, to_right], in3.at[:, to_left], 10, {"space": space(1)}),
        remote(out3.at[:, to_left], in3.at[:, to_right], 11, {"space": space(-1)}),
        remote(out3.at[0, to_right], far3.at[to_left], 12, {"space": space(2)}),
        remote(out3.at[0, to_left], far3.at[to_right], 13, {"space": space(-2)}),
    ]
    for copy in second:
        copy.start()

    fc = gather(sc, gathered)
    base0 = pre0 + (1.0 + DAMPING - sigma) * c + sigma * fc
    base1 = w + pre1 - DAMPING * c + sigma * (fc + timed(c))
    basep = before_carry[...] + KEEP * wp + sigma * (gather(sp, gathered) + timed(wp))
    basep = jnp.where(started, basep, 0.0)
    base1 = v0_1 + KEEP * base1 + sigma * (faces(base1) + timed(base0))
    base0 = v0_0 + KEEP * base0 + sigma * (faces(base0) + timed(basep))

    for copy in second:
        copy.wait()
    st = stacks(jnp.concatenate([in3[0], in3[1]] + seen_by_halo(far3[...], sent_c), axis=0))
    seen = halves(dot(halo_sent, split(st[0])))
    change = sent_sigma * seen
    change_p = sent_sigma * halves(dot(halo_sent, split(st[1])))
    extra = halo_sigma * halves(dot(far_halo, split(jnp.concatenate(st[2:4], axis=0))))
    st = stacks(jnp.concatenate([in3[2] + extra, in3[3] + extra, change], axis=0))
    t = timed(jnp.concatenate([change, change_p], axis=0))
    kept = KEEP * seen
    out_ref[1] = base1 + sigma * scattered(st[1], st[2], kept + t[0:32])
    out_ref[0] = base0 + sigma * scattered(st[0], st[2], kept + t[32:64])


def solution(mesh):
    groups, partitions = mesh.shape["tm"], mesh.shape["space"]

    def body(source, elem_scale, diag_block, block_inverse, face_flux, time_trace, neighbours, send_rows):
        any_space = pl.BlockSpec(memory_space=pl.ANY)
        vmem = pltpu.VMEM
        rows = (256, 128)
        return pl.pallas_call(
            lambda *refs: kernel(groups, partitions, *refs),
            out_shape=jax.ShapeDtypeStruct((2, 256, 128), F32),
            in_specs=[any_space] * 7,
            out_specs=pl.BlockSpec(memory_space=pltpu.VMEM),
            scratch_shapes=[
                vmem((2, 256, 128), F32), vmem((1, 256), F32), vmem((128, 128), F32), vmem((4, 128, 128), F32),
                vmem((128, 128), F32), vmem((4, 256), jnp.int32), vmem((1, 32), jnp.int32),
                vmem((1024, 256), BF16), vmem((256, 384), BF16), vmem((1024, 256), BF16),
                vmem((256, 768), BF16), vmem((256, 768), BF16), vmem((256, 1024), BF16),
                vmem(rows, F32), vmem((5, 32, 128), F32), vmem((5, 32, 128), F32), vmem((2, 32, 128), F32),
                vmem((32, 128), F32), vmem(rows, F32),
                vmem(rows, F32), vmem(rows, F32), vmem(rows, F32), vmem(rows, F32),
                vmem((16 * (groups + 1), 128), F32), vmem((groups, 32, 128), F32),
                vmem((4, 32, 128), F32), vmem((4, 32, 128), F32), vmem((32, 128), F32), vmem(rows, F32),
                pltpu.SemaphoreType.DMA((7,)), pltpu.SemaphoreType.DMA((14,)), pltpu.SemaphoreType.DMA((14,)),
            ],
            compiler_params=pltpu.CompilerParams(
                collective_id=0, has_side_effects=True, vmem_limit_bytes=56 * 1024 * 1024
            ),
        )(source, elem_scale.reshape(1, 256), block_inverse, face_flux, time_trace, neighbours.T, send_rows)

    return jax.shard_map(
        body,
        mesh=mesh,
        in_specs=(P("tm", "space", None), P("space"), P(), P(), P(), P(), P("space", None), P("space", None)),
        out_specs=P("tm", "space", None),
        check_vma=False,
    )
```

time: 46 us -> 38.6 us (0.84)
  local copies, waits for them, and re-layouts: 5.65 us -> 1.67 us
  Pallas kernels: 40 us -> 36.8 us
    unnamed x15 -> x1, local copies, waits for them, and re-layouts: 5.65 us -> 1.67 us
    pallas_call x1, Pallas kernels: 40 us -> 36.8 us  [body(): pl.pallas_call(lambda *refs: kernel(groups, partitions, *refs), out_shape...]
where the time goes in v2:
time: 38.6 us; the launch traced here: 38.5 us
  Pallas kernels  36.8 us (95%)
  local copies, waits for them, and re-layouts  1.67 us (4%)
    pallas_call x1, Pallas kernels, body(): pl.pallas_call(lambda *refs: kernel(groups, partitions, *refs), out_shape...  36.8 us
    unnamed x1, local copies, waits for them, and re-layouts  1.67 us

profile of v2, /device:TPU:1, one launch (start us, length us, event | category | flops | bytes accessed | tf_op | source)
XLA Modules:
  0.0 38.5 jit_solution(6047012092868218150)
XLA Ops:
  0.0 36.8 %shard_map.73 = f32[2,256,128]{2,1,0:T(8,128)} custom-call(f32[2,256,128]{2,1,0:T(8,128)} %refs_0_.1, f32[1,256]{1,0:T(1,128)} %bitcast.3, f32[128,128]{1,0:T(8,128)} %refs_2_.1, f32[4,128,128]{2,1,0:T(8,128)} %refs_3_.1, f32[128,128]{1,0:T(8,128)} %refs_4_.1, s32[4,256]{1,0:T(4,128)} %bitcast.2, s32[1,32]{1,0:T(1,128)} %refs_6_.1), custom_call_target="tpu_custom_call" | custom-call | tf_op jit(solution)/shard_map/pallas_call | solution.py:379
  36.8 1.7 %copy.9 = f32[2,256,128]{2,1,0:T(8,128)} copy(f32[2,256,128]{2,1,0:T(8,128)} %shard_map.73) | data formatting | bytes 524288

commit v3 on v2

--- a/solution.py
+++ b/solution.py
@@ -64,7 +64,7 @@
     out_ref,
     source, scale_row, inverse, flux, trace, neighbours, send_row,
     pick, spread, face_w, near_w, far_w, gathered,
-    v0_last, out1, in1, far1, diag1, before0,
+    v0_last, out1, in1, far1, before0,
     rhs, rhs_all, carry, before_carry, chain_out, chain_all, out3, in3, far3, scale_full,
     in_sem, send_sem, recv_sem,
 ):
@@ -92,12 +92,10 @@
                 if min(dy, 4 - dy) + min(dx, 4 - dx) == hops:
                     others.append(lax.rem(k // 4 + dy, 4) * 4 + lax.rem(lax.rem(k, 4) + dx, 4))
     after = lax.rem(k + 1, groups)
-    ahead = lax.rem(k + groups - 1, groups)
 
     barrier = pltpu.get_barrier_semaphore()
     senders = [{"tm": other} for other in others]
     senders += [{"space": space(by)} for by in (1, -1, 2, -2)]
-    senders += [{"tm": ahead, "space": space(by)} for by in (1, -1)]
     for partner in senders:
         pl.semaphore_signal(barrier, inc=1, device_id=partner, device_id_type=MESH)
 
@@ -173,7 +171,7 @@
 
     out1[2] = (1.0 + KEEP) * own0 + sent_sigma * sent_faces(s0)
     out1[3] = (1.0 + KEEP) * own1 + sent_sigma * (sent_faces(s1) + timed(own0))
-    pl.semaphore_wait(barrier, groups + 5)
+    pl.semaphore_wait(barrier, groups + 3)
 
     to_right, to_left = pl.ds(16, 16), pl.ds(0, 16)
     first = [
@@ -181,10 +179,8 @@
         remote(out1.at[:, to_left], in1.at[:, to_right], 1, {"space": space(-1)}),
         remote(out1.at[0:2, to_right], far1.at[:, to_left], 2, {"space": space(2)}),
         remote(out1.at[0:2, to_left], far1.at[:, to_right], 3, {"space": space(-2)}),
-        remote(out1.at[1, to_right], diag1.at[to_left], 4, {"tm": after, "space": space(1)}),
-        remote(out1.at[1, to_left], diag1.at[to_right], 5, {"tm": after, "space": space(-1)}),
     ]
-    first_last = remote(v0_last, before0, 6, {"tm": after})
+    first_last = remote(v0_last, before0, 4, {"tm": after})
     for copy in first + [first_last]:
         copy.start()
 
@@ -227,6 +223,8 @@
     base0 = (1.0 + KEEP) * v0_0 + sigma * gather(s0, gathered)
     rest1 = a1 - scale * base1 + faces(base1) + timed(base0)
     rest0 = a0 - scale * base0 + faces(base0)
+    onward = sigma * timed(v0_1)
+    onward = faces(onward) + timed(onward) - scale * onward
 
     for copy in first:
         copy.wait()
@@ -246,38 +244,38 @@
     )
     change0 = sent_sigma * halves(dot(halo_sent, split(st[0])))
     change1 = sent_sigma * halves(dot(halo_sent, split(st[1])))
-    halo_v0 = in1[2] + halo_sigma * (
-        halves(dot(far_halo, split(jnp.concatenate(st[2:4], axis=0)))) + timed(jnp.where(started, diag1[...], 0.0))
-    )
+    halo_v0 = in1[2] + halo_sigma * halves(dot(far_halo, split(jnp.concatenate(st[2:4], axis=0))))
     halo_v1 = in1[3] + halo_sigma * halves(dot(far_halo, split(jnp.concatenate(st[4:6], axis=0))))
-    st = stacks(jnp.concatenate([halo_v0, halo_v1, change0, change1], axis=0))
-    rest1 = rest1 + scattered(st[1], st[3], timed(change0) - sent_scale * change1)
-    rest0 = rest0 + scattered(st[0], st[2], -sent_scale * change0)
+    change = change0 + change1
+    t_change0 = timed(change0)
+    st = stacks(jnp.concatenate([halo_v0 + halo_v1, change, halo_sigma * timed(in1[1])], axis=0))
+    total = rest0 + rest1 + scattered(st[0], st[1], t_change0 - sent_scale * change)
+    onward = onward + halves(dot(spread[:, 0:128], split(st[2])))
     place = spread[:, 256:384]
     rest = jnp.zeros((96, 128), F32)
     v1_1 = base1 + halves(dot(place, split(jnp.concatenate([change1, rest], axis=0))))
+    rhs[:, 0:16] = (coarse * total + v1_1).reshape(groups, 16, 128)
+    rhs[:, 16:32] = (coarse * onward).reshape(groups, 16, 128)
+    mine = pl.ds(pl.multiple_of(k * 16, 16), 16)
+
+    def block(i, size=16):
+        return pl.ds(pl.multiple_of(i * 16, 16), size)
+
+    for other in others:
+        remote(rhs.at[other], rhs_all.at[k], 5, {"tm": other}).start()
+    count = pl.ds(0, groups - 1)
+    to_owners = remote(rhs.at[count], rhs_all.at[count], 5, {"tm": after})
+    rhs_all[k] = rhs[k]
+
+    st = stacks(jnp.concatenate([halo_v1, change1], axis=0))
+    rest1 = rest1 + scattered(st[0], st[1], t_change0 - sent_scale * change1)
     base0 = base0 + halves(dot(place, split(jnp.concatenate([change0, rest], axis=0))))
-    ready = coarse * (rest0 + rest1) + v1_1
-
     first_last.wait()
     delta = sigma * timed(jnp.where(started, before0[...], 0.0))
-    t_delta = timed(delta)
-    rhs[...] = ready + coarse * (faces(delta) + t_delta - scale * delta)
-    mine = pl.ds(pl.multiple_of(k * 16, 16), 16)
-
-    def block(i, size=16):
-        return pl.ds(pl.multiple_of(i * 16, 16), size)
-
-    for other in others:
-        remote(rhs.at[block(other)], rhs_all.at[mine], 7, {"tm": other}).start()
-    count = pl.ds(0, 16 * (groups - 1))
-    to_owners = remote(rhs.at[count], rhs_all.at[count], 7, {"tm": after})
-    rhs_all[mine, :] = rhs[mine, :]
-
     v1_0 = base0 + delta
-    step = sigma * (rest1 + t_delta)
+    step = sigma * (rest1 + timed(delta))
     carry[...] = v0_1 + sigma * timed(v1_0 - v1_1)
-    carried = remote(carry, before_carry, 8, {"tm": after})
+    carried = remote(carry, before_carry, 6, {"tm": after})
     carried.start()
     pre0 = v1_0 - step
     pre1 = v1_1 + step
@@ -305,7 +303,7 @@
     chain_out[0:16, :] = jnp.zeros((16, 128), F32)
 
     to_owners.wait()
-    x = rhs_all[...]
+    x = rhs_all[:, 0:16].reshape(256, 128) + later(rhs_all[:, 16:32].reshape(256, 128), 1)
     y = dot(split(x), near_w[...])
     x = (
         x
@@ -321,8 +319,8 @@
         + later(c4 * c8 * halves(y[:, 512:768]), 12)
     )
     for other in others:
-        remote(chain_out.at[block(other, 32)], chain_all.at[k], 9, {"tm": other}).start()
-    to_slabs = remote(chain_all.at[pl.ds(0, groups - 1)], chain_all.at[pl.ds(0, groups - 1)], 9, {"tm": after})
+        remote(chain_out.at[block(other, 32)], chain_all.at[k], 7, {"tm": other}).start()
+    to_slabs = remote(chain_all.at[count], chain_all.at[count], 7, {"tm": after})
     chain_all[k] = chain_out[block(k, 32), :]
     for copy in (to_slabs, carried):
         copy.wait()
@@ -339,10 +337,10 @@
     out3[2] = sent_pre0 + (1.0 + DAMPING - sent_sigma) * sent_c + sent_sigma * sent_fc
     out3[3] = sent_pre1 + KEEP * sent_c + sent_sigma * (sent_fc + timed(sent_c))
     second = [
-        remote(out3.at[:, to_right], in3.at[:, to_left], 10, {"space": space(1)}),
-        remote(out3.at[:, to_left], in3.at[:, to_right], 11, {"space": space(-1)}),
-        remote(out3.at[0, to_right], far3.at[to_left], 12, {"space": space(2)}),
-        remote(out3.at[0, to_left], far3.at[to_right], 13, {"space": space(-2)}),
+        remote(out3.at[:, to_right], in3.at[:, to_left], 8, {"space": space(1)}),
+        remote(out3.at[:, to_left], in3.at[:, to_right], 9, {"space": space(-1)}),
+        remote(out3.at[0, to_right], far3.at[to_left], 10, {"space": space(2)}),
+        remote(out3.at[0, to_left], far3.at[to_right], 11, {"space": space(-2)}),
     ]
     for copy in second:
         copy.start()
@@ -387,16 +385,16 @@
                 vmem((1024, 256), BF16), vmem((256, 384), BF16), vmem((1024, 256), BF16),
                 vmem((256, 768), BF16), vmem((256, 768), BF16), vmem((256, 1024), BF16),
                 vmem(rows, F32), vmem((5, 32, 128), F32), vmem((5, 32, 128), F32), vmem((2, 32, 128), F32),
-                vmem((32, 128), F32), vmem(rows, F32),
-                vmem(rows, F32), vmem(rows, F32), vmem(rows, F32), vmem(rows, F32),
+                vmem(rows, F32),
+                vmem((groups, 32, 128), F32), vmem((groups, 32, 128), F32), vmem(rows, F32), vmem(rows, F32),
                 vmem((16 * (groups + 1), 128), F32), vmem((groups, 32, 128), F32),
                 vmem((4, 32, 128), F32), vmem((4, 32, 128), F32), vmem((32, 128), F32), vmem(rows, F32),
-                pltpu.SemaphoreType.DMA((7,)), pltpu.SemaphoreType.DMA((14,)), pltpu.SemaphoreType.DMA((14,)),
+                pltpu.SemaphoreType.DMA((7,)), pltpu.SemaphoreType.DMA((12,)), pltpu.SemaphoreType.DMA((12,)),
             ],
             compiler_params=pltpu.CompilerParams(
-                collective_id=0, has_side_effects=True, vmem_limit_bytes=56 * 1024 * 1024
+                collective_id=0, has_side_effects=True, vmem_limit_bytes=32 * 1024 * 1024
             ),
-        )(source, elem_scale.reshape(1, 256), block_inverse, face_flux, time_trace, neighbours.T, send_rows)
+        )(*[pltpu.with_memory_space_constraint(x, pltpu.HBM) for x in (source, elem_scale.reshape(1, 256), block_inverse, face_flux, time_trace, neighbours.T, send_rows)])
 
     return jax.shard_map(
         body,

time: 38.6 us -> 36.4 us (0.943)
  Pallas kernels: 36.8 us -> 35.5 us
  local copies, waits for them, and re-layouts: 1.67 us -> 0.71 us
    pallas_call x1, Pallas kernels: 36.8 us -> 35.5 us  [body(): pl.pallas_call(lambda *refs: kernel(groups, partitions, *refs), out_shape...]
    unnamed x1, local copies, waits for them, and re-layouts: 1.67 us -> 0.71 us
where the time goes in v3:
time: 36.4 us; the launch traced here: 36.2 us
  Pallas kernels  35.5 us (98%)
  local copies, waits for them, and re-layouts  0.71 us (2%)
    pallas_call x1, Pallas kernels, body(): pl.pallas_call(lambda *refs: kernel(groups, partitions, *refs), out_shape...  35.5 us

profile of v3, /device:TPU:1, one launch (start us, length us, event | category | flops | bytes accessed | tf_op | source)
XLA Modules:
  0.0 36.2 jit_solution(6794688375080802164)
XLA Ops:
  0.0 35.5 %shard_map.73 = f32[2,256,128]{2,1,0:T(8,128)S(1)} custom-call(f32[2,256,128]{2,1,0:T(8,128)} %refs_0_.1, f32[1,256]{1,0:T(1,128)} %bitcast.3, f32[128,128]{1,0:T(8,128)} %refs_2_.1, f32[4,128,128]{2,1,0:T(8,128)} %refs_3_.1, f32[128,128]{1,0:T(8,128)} %refs_4_.1, s32[4,256]{1,0:T(4,128)} %bitcast.2, s32[1,32]{1,0:T(1,128)} %refs_6_.1), custom_call_target="tpu_custom_call" | custom-call | tf_op jit(solution)/shard_map/pallas_call | solution.py:377
  35.5 0.7 %copy.9 = f32[2,256,128]{2,1,0:T(8,128)} copy(f32[2,256,128]{2,1,0:T(8,128)S(1)} %shard_map.73) | data formatting | bytes 524288

commit v4 on v3

--- a/solution.py
+++ b/solution.py
@@ -227,7 +227,7 @@
     onward = faces(onward) + timed(onward) - scale * onward
 
     for copy in first:
-        copy.wait()
+        copy.wait_recv()
     started = k > 0
     facts = in1[4]
     far_names = [facts[:, f : f + 1] for f in range(4)]
@@ -270,13 +270,12 @@
     st = stacks(jnp.concatenate([halo_v1, change1], axis=0))
     rest1 = rest1 + scattered(st[0], st[1], t_change0 - sent_scale * change1)
     base0 = base0 + halves(dot(place, split(jnp.concatenate([change0, rest], axis=0))))
-    first_last.wait()
+    first_last.wait_recv()
     delta = sigma * timed(jnp.where(started, before0[...], 0.0))
     v1_0 = base0 + delta
     step = sigma * (rest1 + timed(delta))
     carry[...] = v0_1 + sigma * timed(v1_0 - v1_1)
     carried = remote(carry, before_carry, 6, {"tm": after})
-    carried.start()
     pre0 = v1_0 - step
     pre1 = v1_1 + step
     sent_pre0 = chosen(pre0)
@@ -302,7 +301,7 @@
     c8 = c4 * c4
     chain_out[0:16, :] = jnp.zeros((16, 128), F32)
 
-    to_owners.wait()
+    to_owners.wait_recv()
     x = rhs_all[:, 0:16].reshape(256, 128) + later(rhs_all[:, 16:32].reshape(256, 128), 1)
     y = dot(split(x), near_w[...])
     x = (
@@ -322,8 +321,9 @@
         remote(chain_out.at[block(other, 32)], chain_all.at[k], 7, {"tm": other}).start()
     to_slabs = remote(chain_all.at[count], chain_all.at[count], 7, {"tm": after})
     chain_all[k] = chain_out[block(k, 32), :]
-    for copy in (to_slabs, carried):
-        copy.wait()
+    to_slabs.wait_send()
+    carried.start()
+    to_slabs.wait_recv()
 
     w = chain_all[:, 16:32].reshape(256, 128)
     wp = chain_all[:, 0:16].reshape(256, 128)
@@ -348,13 +348,14 @@
     fc = gather(sc, gathered)
     base0 = pre0 + (1.0 + DAMPING - sigma) * c + sigma * fc
     base1 = w + pre1 - DAMPING * c + sigma * (fc + timed(c))
+    carried.wait_recv()
     basep = before_carry[...] + KEEP * wp + sigma * (gather(sp, gathered) + timed(wp))
     basep = jnp.where(started, basep, 0.0)
     base1 = v0_1 + KEEP * base1 + sigma * (faces(base1) + timed(base0))
     base0 = v0_0 + KEEP * base0 + sigma * (faces(base0) + timed(basep))
 
     for copy in second:
-        copy.wait()
+        copy.wait_recv()
     st = stacks(jnp.concatenate([in3[0], in3[1]] + seen_by_halo(far3[...], sent_c), axis=0))
     seen = halves(dot(halo_sent, split(st[0])))
     change = sent_sigma * seen
@@ -365,6 +366,8 @@
     kept = KEEP * seen
     out_ref[1] = base1 + sigma * scattered(st[1], st[2], kept + t[0:32])
     out_ref[0] = base0 + sigma * scattered(st[0], st[2], kept + t[32:64])
+    for copy in first + [first_last, to_owners, carried] + second:
+        copy.wait_send()
 
 
 def solution(mesh):

time: 36.4 us -> 35.5 us (0.975)
  Pallas kernels: 35.5 us -> 34.7 us
    pallas_call x1, Pallas kernels: 35.5 us -> 34.7 us  [body(): pl.pallas_call(lambda *refs: kernel(groups, partitions, *refs), out_shape...]
where the time goes in v4:
time: 35.5 us; the launch traced here: 35.4 us
  Pallas kernels  34.7 us (98%)
  local copies, waits for them, and re-layouts  0.71 us (2%)
    pallas_call x1, Pallas kernels, body(): pl.pallas_call(lambda *refs: kernel(groups, partitions, *refs), out_shape...  34.7 us

profile of v4, /device:TPU:1, one launch (start us, length us, event | category | flops | bytes accessed | tf_op | source)
XLA Modules:
  0.0 35.4 jit_solution(18095680477169882981)
XLA Ops:
  0.0 34.7 %shard_map.73 = f32[2,256,128]{2,1,0:T(8,128)S(1)} custom-call(f32[2,256,128]{2,1,0:T(8,128)} %refs_0_.1, f32[1,256]{1,0:T(1,128)} %bitcast.3, f32[128,128]{1,0:T(8,128)} %refs_2_.1, f32[4,128,128]{2,1,0:T(8,128)} %refs_3_.1, f32[128,128]{1,0:T(8,128)} %refs_4_.1, s32[4,256]{1,0:T(4,128)} %bitcast.2, s32[1,32]{1,0:T(1,128)} %refs_6_.1), custom_call_target="tpu_custom_call" | custom-call | tf_op jit(solution)/shard_map/pallas_call | solution.py:380
  34.7 0.7 %copy.9 = f32[2,256,128]{2,1,0:T(8,128)} copy(f32[2,256,128]{2,1,0:T(8,128)S(1)} %shard_map.73) | data formatting | bytes 524288

commit v5 on v4

--- a/solution.py
+++ b/solution.py
@@ -66,7 +66,7 @@
     pick, spread, face_w, near_w, far_w, gathered,
     v0_last, out1, in1, far1, before0,
     rhs, rhs_all, carry, before_carry, chain_out, chain_all, out3, in3, far3, scale_full,
-    in_sem, send_sem, recv_sem,
+    in_sem, send_sem, recv_sem, greet_sem,
 ):
     k = lax.axis_index("tm")
     p = lax.axis_index("space")
@@ -79,9 +79,6 @@
             ]
         )
     ]
-    for load in loads:
-        load.start()
-
     def space(by):
         return lax.rem(p + partitions + by, partitions)
 
@@ -94,10 +91,14 @@
     after = lax.rem(k + 1, groups)
 
     barrier = pltpu.get_barrier_semaphore()
-    senders = [{"tm": other} for other in others]
-    senders += [{"space": space(by)} for by in (1, -1, 2, -2)]
+    beside = [{"tm": k // 4 * 4 + lax.rem(lax.rem(k, 4) + by, 4)} for by in (2, 1, 3)]
+    along = [{"tm": lax.rem(k + by, groups)} for by in (8, 4, 12)]
+    senders = [{"tm": lax.rem(k + groups - 1, groups)}] + beside + along
+    senders += [{"space": space(by)} for by in (2, -2, 1, -1)]
     for partner in senders:
         pl.semaphore_signal(barrier, inc=1, device_id=partner, device_id_type=MESH)
+    for load in loads:
+        load.start()
 
     def remote(src, dst, number, device):
         return pltpu.make_async_remote_copy(
@@ -136,7 +137,7 @@
     facts = jnp.where(lane == 4, sent_sigma, 0.0)
     for f in range(4):
         facts = facts + jnp.where(lane == f, sent_names[f], 0.0)
-    out1[4] = facts
+    out1[3] = facts
 
     loads[3].wait()
     inverse_w = weights(inverse[...])
@@ -169,20 +170,32 @@
         rows = jnp.concatenate([rows[f * 32 : (f + 1) * 32] for f in range(4)], axis=1)
         return halves(dot(rows, face_w[...]))
 
-    out1[2] = (1.0 + KEEP) * own0 + sent_sigma * sent_faces(s0)
-    out1[3] = (1.0 + KEEP) * own1 + sent_sigma * (sent_faces(s1) + timed(own0))
-    pl.semaphore_wait(barrier, groups + 3)
+    part1 = (1.0 + KEEP) * own1 + sent_sigma * (sent_faces(s1) + timed(own0))
+    own_sum = own0 + own1
+    out1[2] = part1 + (1.0 + KEEP) * own0 + sent_sigma * sent_faces(s0)
+    out1[4] = part1
+    out1[5] = own_sum
+    pl.semaphore_wait(barrier, 11)
 
     to_right, to_left = pl.ds(16, 16), pl.ds(0, 16)
     first = [
-        remote(out1.at[:, to_right], in1.at[:, to_left], 0, {"space": space(1)}),
-        remote(out1.at[:, to_left], in1.at[:, to_right], 1, {"space": space(-1)}),
-        remote(out1.at[0:2, to_right], far1.at[:, to_left], 2, {"space": space(2)}),
-        remote(out1.at[0:2, to_left], far1.at[:, to_right], 3, {"space": space(-2)}),
+        remote(out1.at[0:4, to_right], in1.at[0:4, to_left], 0, {"space": space(1)}),
+        remote(out1.at[0:4, to_left], in1.at[0:4, to_right], 1, {"space": space(-1)}),
+        remote(out1.at[5, to_right], far1.at[0, to_left], 2, {"space": space(2)}),
+        remote(out1.at[5, to_left], far1.at[0, to_right], 3, {"space": space(-2)}),
     ]
-    first_last = remote(v0_last, before0, 4, {"tm": after})
-    for copy in first + [first_last]:
+    late = [
+        remote(out1.at[4, to_right], in1.at[4, to_left], 6, {"space": space(1)}),
+        remote(out1.at[4, to_left], in1.at[4, to_right], 7, {"space": space(-1)}),
+        remote(out1.at[1, to_right], far1.at[1, to_left], 8, {"space": space(2)}),
+        remote(out1.at[1, to_left], far1.at[1, to_right], 9, {"space": space(-2)}),
+    ]
+    first_last = remote(v0_last, before0, 10, {"tm": after})
+    for copy in first + late + [first_last]:
         copy.start()
+
+    for partner in along:
+        pl.semaphore_signal(greet_sem, inc=1, device_id=partner, device_id_type=MESH)
 
     send4 = jnp.concatenate([send_col] * 4, axis=0)
     eye = iota((128, 128), 0) == iota((128, 128), 1)
@@ -219,6 +232,11 @@
     def chosen(x):
         return halves(dot(choose, split(x)))
 
+    mine = pl.ds(pl.multiple_of(k * 16, 16), 16)
+
+    def block(i, size=16):
+        return pl.ds(pl.multiple_of(i * 16, 16), size)
+
     base1 = (1.0 + KEEP) * v0_1 + sigma * (gather(s1, gathered) + timed(v0_0))
     base0 = (1.0 + KEEP) * v0_0 + sigma * gather(s0, gathered)
     rest1 = a1 - scale * base1 + faces(base1) + timed(base0)
@@ -229,7 +247,7 @@
     for copy in first:
         copy.wait_recv()
     started = k > 0
-    facts = in1[4]
+    facts = in1[3]
     far_names = [facts[:, f : f + 1] for f in range(4)]
     halo_sigma = facts[:, 4:5]
     far_hits = halo_hits(far_names, 32).astype(F32)
@@ -239,16 +257,13 @@
     def seen_by_halo(far, own):
         return [far[0:16], own[0:16], own[16:32], far[16:32]]
 
-    st = stacks(
-        jnp.concatenate([in1[0], in1[1]] + seen_by_halo(far1[0], own0) + seen_by_halo(far1[1], own1), axis=0)
-    )
+    st = stacks(jnp.concatenate([in1[0], in1[1]] + seen_by_halo(far1[0], own_sum), axis=0))
     change0 = sent_sigma * halves(dot(halo_sent, split(st[0])))
     change1 = sent_sigma * halves(dot(halo_sent, split(st[1])))
-    halo_v0 = in1[2] + halo_sigma * halves(dot(far_halo, split(jnp.concatenate(st[2:4], axis=0))))
-    halo_v1 = in1[3] + halo_sigma * halves(dot(far_halo, split(jnp.concatenate(st[4:6], axis=0))))
+    halo_sum = in1[2] + halo_sigma * halves(dot(far_halo, split(jnp.concatenate(st[2:4], axis=0))))
     change = change0 + change1
     t_change0 = timed(change0)
-    st = stacks(jnp.concatenate([halo_v0 + halo_v1, change, halo_sigma * timed(in1[1])], axis=0))
+    st = stacks(jnp.concatenate([halo_sum, change, halo_sigma * timed(in1[1])], axis=0))
     total = rest0 + rest1 + scattered(st[0], st[1], t_change0 - sent_scale * change)
     onward = onward + halves(dot(spread[:, 0:128], split(st[2])))
     place = spread[:, 256:384]
@@ -256,17 +271,16 @@
     v1_1 = base1 + halves(dot(place, split(jnp.concatenate([change1, rest], axis=0))))
     rhs[:, 0:16] = (coarse * total + v1_1).reshape(groups, 16, 128)
     rhs[:, 16:32] = (coarse * onward).reshape(groups, 16, 128)
-    mine = pl.ds(pl.multiple_of(k * 16, 16), 16)
-
-    def block(i, size=16):
-        return pl.ds(pl.multiple_of(i * 16, 16), size)
-
+    pl.semaphore_wait(greet_sem, 3)
     for other in others:
-        remote(rhs.at[other], rhs_all.at[k], 5, {"tm": other}).start()
-    count = pl.ds(0, groups - 1)
-    to_owners = remote(rhs.at[count], rhs_all.at[count], 5, {"tm": after})
+        remote(rhs.at[other], rhs_all.at[k], 12, {"tm": other}).start()
+    to_owners = remote(rhs.at[0 : groups - 1], rhs_all.at[0 : groups - 1], 12, {"tm": after})
     rhs_all[k] = rhs[k]
 
+    for copy in late:
+        copy.wait_recv()
+    st = stacks(jnp.concatenate(seen_by_halo(far1[1], own1), axis=0))
+    halo_v1 = in1[4] + halo_sigma * halves(dot(far_halo, split(jnp.concatenate(st, axis=0))))
     st = stacks(jnp.concatenate([halo_v1, change1], axis=0))
     rest1 = rest1 + scattered(st[0], st[1], t_change0 - sent_scale * change1)
     base0 = base0 + halves(dot(place, split(jnp.concatenate([change0, rest], axis=0))))
@@ -275,7 +289,7 @@
     v1_0 = base0 + delta
     step = sigma * (rest1 + timed(delta))
     carry[...] = v0_1 + sigma * timed(v1_0 - v1_1)
-    carried = remote(carry, before_carry, 6, {"tm": after})
+    carried = remote(carry, before_carry, 13, {"tm": after})
     pre0 = v1_0 - step
     pre1 = v1_1 + step
     sent_pre0 = chosen(pre0)
@@ -318,8 +332,8 @@
         + later(c4 * c8 * halves(y[:, 512:768]), 12)
     )
     for other in others:
-        remote(chain_out.at[block(other, 32)], chain_all.at[k], 7, {"tm": other}).start()
-    to_slabs = remote(chain_all.at[count], chain_all.at[count], 7, {"tm": after})
+        remote(chain_out.at[block(other, 32)], chain_all.at[k], 14, {"tm": other}).start()
+    to_slabs = remote(chain_all.at[0 : groups - 1], chain_all.at[0 : groups - 1], 14, {"tm": after})
     chain_all[k] = chain_out[block(k, 32), :]
     to_slabs.wait_send()
     carried.start()
@@ -337,10 +351,10 @@
     out3[2] = sent_pre0 + (1.0 + DAMPING - sent_sigma) * sent_c + sent_sigma * sent_fc
     out3[3] = sent_pre1 + KEEP * sent_c + sent_sigma * (sent_fc + timed(sent_c))
     second = [
-        remote(out3.at[:, to_right], in3.at[:, to_left], 8, {"space": space(1)}),
-        remote(out3.at[:, to_left], in3.at[:, to_right], 9, {"space": space(-1)}),
-        remote(out3.at[0, to_right], far3.at[to_left], 10, {"space": space(2)}),
-        remote(out3.at[0, to_left], far3.at[to_right], 11, {"space": space(-2)}),
+        remote(out3.at[:, to_right], in3.at[:, to_left], 15, {"space": space(1)}),
+        remote(out3.at[:, to_left], in3.at[:, to_right], 16, {"space": space(-1)}),
+        remote(out3.at[0, to_right], far3.at[to_left], 17, {"space": space(2)}),
+        remote(out3.at[0, to_left], far3.at[to_right], 18, {"space": space(-2)}),
     ]
     for copy in second:
         copy.start()
@@ -366,7 +380,7 @@
     kept = KEEP * seen
     out_ref[1] = base1 + sigma * scattered(st[1], st[2], kept + t[0:32])
     out_ref[0] = base0 + sigma * scattered(st[0], st[2], kept + t[32:64])
-    for copy in first + [first_last, to_owners, carried] + second:
+    for copy in first + late + [first_last, to_owners, carried] + second:
         copy.wait_send()
 
 
@@ -387,12 +401,13 @@
                 vmem((128, 128), F32), vmem((4, 256), jnp.int32), vmem((1, 32), jnp.int32),
                 vmem((1024, 256), BF16), vmem((256, 384), BF16), vmem((1024, 256), BF16),
                 vmem((256, 768), BF16), vmem((256, 768), BF16), vmem((256, 1024), BF16),
-                vmem(rows, F32), vmem((5, 32, 128), F32), vmem((5, 32, 128), F32), vmem((2, 32, 128), F32),
+                vmem(rows, F32), vmem((6, 32, 128), F32), vmem((5, 32, 128), F32), vmem((2, 32, 128), F32),
                 vmem(rows, F32),
                 vmem((groups, 32, 128), F32), vmem((groups, 32, 128), F32), vmem(rows, F32), vmem(rows, F32),
                 vmem((16 * (groups + 1), 128), F32), vmem((groups, 32, 128), F32),
                 vmem((4, 32, 128), F32), vmem((4, 32, 128), F32), vmem((32, 128), F32), vmem(rows, F32),
-                pltpu.SemaphoreType.DMA((7,)), pltpu.SemaphoreType.DMA((12,)), pltpu.SemaphoreType.DMA((12,)),
+                pltpu.SemaphoreType.DMA((7,)), pltpu.SemaphoreType.DMA((19,)), pltpu.SemaphoreType.DMA((19,)),
+                pltpu.SemaphoreType.REGULAR,
             ],
             compiler_params=pltpu.CompilerParams(
                 collective_id=0, has_side_effects=True, vmem_limit_bytes=32 * 1024 * 1024

time: 35.5 us -> 34.1 us (0.961)
  Pallas kernels: 34.7 us -> 33.3 us
    pallas_call x1, Pallas kernels: 34.7 us -> 33.3 us  [body(): pl.pallas_call(lambda *refs: kernel(groups, partitions, *refs), out_shape...]
where the time goes in v5:
time: 34.1 us; the launch traced here: 34 us
  Pallas kernels  33.3 us (98%)
  local copies, waits for them, and re-layouts  0.71 us (2%)
    pallas_call x1, Pallas kernels, body(): pl.pallas_call(lambda *refs: kernel(groups, partitions, *refs), out_shape...  33.3 us
    unnamed x1, local copies, waits for them, and re-layouts  0.71 us

profile of v5, /device:TPU:1, one launch (start us, length us, event | category | flops | bytes accessed | tf_op | source)
XLA Modules:
  0.0 34.0 jit_solution(11560258080217603168)
XLA Ops:
  0.0 33.3 %shard_map.73 = f32[2,256,128]{2,1,0:T(8,128)S(1)} custom-call(f32[2,256,128]{2,1,0:T(8,128)} %refs_0_.1, f32[1,256]{1,0:T(1,128)} %bitcast.3, f32[128,128]{1,0:T(8,128)} %refs_2_.1, f32[4,128,128]{2,1,0:T(8,128)} %refs_3_.1, f32[128,128]{1,0:T(8,128)} %refs_4_.1, s32[4,256]{1,0:T(4,128)} %bitcast.2, s32[1,32]{1,0:T(1,128)} %refs_6_.1), custom_call_target="tpu_custom_call" | custom-call | tf_op jit(solution)/shard_map/pallas_call | solution.py:394
  33.3 0.7 %copy.9 = f32[2,256,128]{2,1,0:T(8,128)} copy(f32[2,256,128]{2,1,0:T(8,128)S(1)} %shard_map.73) | data formatting | bytes 524288

commit v6 on v5

--- a/solution.py
+++ b/solution.py
@@ -165,10 +165,13 @@
     def timed(x):
         return halves(dot(split(x), near_w[:, 0:256]))
 
-    def sent_faces(parts):
-        rows = dot(sent_pick, parts).astype(BF16)
+    def named(rows):
+        rows = rows.astype(BF16)
         rows = jnp.concatenate([rows[f * 32 : (f + 1) * 32] for f in range(4)], axis=1)
         return halves(dot(rows, face_w[...]))
+
+    def sent_faces(parts):
+        return named(dot(sent_pick, parts))
 
     part1 = (1.0 + KEEP) * own1 + sent_sigma * (sent_faces(s1) + timed(own0))
     own_sum = own0 + own1
@@ -209,14 +212,14 @@
     element = iota((256, 128), 0).astype(F32)
     spread[:, 256:384] = onehot(jnp.where(lane < 32, send4, -1.0) == element)
 
-    def gather(parts, ref):
+    def gather(parts, slot):
         for f in range(4):
             rows = dot(pick[f * 256 : (f + 1) * 256, :], parts)
-            ref[:, f * 256 : (f + 1) * 256] = rows.astype(BF16)
-        return halves(dot(ref[...], face_w[...]))
-
-    def faces(x):
-        return gather(split(x), gathered)
+            gathered[slot, :, f * 256 : (f + 1) * 256] = rows.astype(BF16)
+        return halves(dot(gathered[slot], face_w[...]))
+
+    def faces(x, slot):
+        return gather(split(x), slot)
 
     def stacks(rows):
         parts = split(rows)
@@ -237,12 +240,13 @@
     def block(i, size=16):
         return pl.ds(pl.multiple_of(i * 16, 16), size)
 
-    base1 = (1.0 + KEEP) * v0_1 + sigma * (gather(s1, gathered) + timed(v0_0))
-    base0 = (1.0 + KEEP) * v0_0 + sigma * gather(s0, gathered)
-    rest1 = a1 - scale * base1 + faces(base1) + timed(base0)
-    rest0 = a0 - scale * base0 + faces(base0)
+    base1 = (1.0 + KEEP) * v0_1 + sigma * (gather(s1, 0) + timed(v0_0))
+    base0 = (1.0 + KEEP) * v0_0 + sigma * gather(s0, 1)
+    rest1 = a1 - scale * base1 + faces(base1, 2) + timed(base0)
+    rest0 = a0 - scale * base0 + faces(base0, 3)
     onward = sigma * timed(v0_1)
-    onward = faces(onward) + timed(onward) - scale * onward
+    onward = coarse * (faces(onward, 4) + timed(onward) - scale * onward)
+    ready = coarse * (rest0 + rest1) + base1
 
     for copy in first:
         copy.wait_recv()
@@ -264,13 +268,10 @@
     change = change0 + change1
     t_change0 = timed(change0)
     st = stacks(jnp.concatenate([halo_sum, change, halo_sigma * timed(in1[1])], axis=0))
-    total = rest0 + rest1 + scattered(st[0], st[1], t_change0 - sent_scale * change)
-    onward = onward + halves(dot(spread[:, 0:128], split(st[2])))
-    place = spread[:, 256:384]
-    rest = jnp.zeros((96, 128), F32)
-    v1_1 = base1 + halves(dot(place, split(jnp.concatenate([change1, rest], axis=0))))
-    rhs[:, 0:16] = (coarse * total + v1_1).reshape(groups, 16, 128)
-    rhs[:, 16:32] = (coarse * onward).reshape(groups, 16, 128)
+    own_rows = t_change0 - sent_scale * change + (2.0 * sent_scale - 1.0) * change1
+    rhs[:, 0:16] = (ready + coarse * scattered(st[0], st[1], own_rows)).reshape(groups, 16, 128)
+    onward = onward + coarse * halves(dot(spread[:, 0:128], split(st[2])))
+    rhs[:, 16:32] = onward.reshape(groups, 16, 128)
     pl.semaphore_wait(greet_sem, 3)
     for other in others:
         remote(rhs.at[other], rhs_all.at[k], 12, {"tm": other}).start()
@@ -281,6 +282,9 @@
         copy.wait_recv()
     st = stacks(jnp.concatenate(seen_by_halo(far1[1], own1), axis=0))
     halo_v1 = in1[4] + halo_sigma * halves(dot(far_halo, split(jnp.concatenate(st, axis=0))))
+    place = spread[:, 256:384]
+    rest = jnp.zeros((96, 128), F32)
+    v1_1 = base1 + halves(dot(place, split(jnp.concatenate([change1, rest], axis=0))))
     st = stacks(jnp.concatenate([halo_v1, change1], axis=0))
     rest1 = rest1 + scattered(st[0], st[1], t_change0 - sent_scale * change1)
     base0 = base0 + halves(dot(place, split(jnp.concatenate([change0, rest], axis=0))))
@@ -344,8 +348,9 @@
     c = w - v1_1
     sc = split(c)
     sp = split(wp)
-    sent_c = halves(dot(choose, sc))
-    sent_fc = sent_faces(sc)
+    rows = dot(jnp.concatenate([sent_pick, choose], axis=0), sc)
+    sent_c = halves(rows[128:160])
+    sent_fc = named(rows[0:128])
     out3[0] = sent_c
     out3[1] = halves(dot(choose, sp))
     out3[2] = sent_pre0 + (1.0 + DAMPING - sent_sigma) * sent_c + sent_sigma * sent_fc
@@ -359,14 +364,14 @@
     for copy in second:
         copy.start()
 
-    fc = gather(sc, gathered)
+    fc = gather(sc, 5)
     base0 = pre0 + (1.0 + DAMPING - sigma) * c + sigma * fc
     base1 = w + pre1 - DAMPING * c + sigma * (fc + timed(c))
     carried.wait_recv()
-    basep = before_carry[...] + KEEP * wp + sigma * (gather(sp, gathered) + timed(wp))
+    basep = before_carry[...] + KEEP * wp + sigma * (gather(sp, 6) + timed(wp))
     basep = jnp.where(started, basep, 0.0)
-    base1 = v0_1 + KEEP * base1 + sigma * (faces(base1) + timed(base0))
-    base0 = v0_0 + KEEP * base0 + sigma * (faces(base0) + timed(basep))
+    base1 = v0_1 + KEEP * base1 + sigma * (faces(base1, 7) + timed(base0))
+    base0 = v0_0 + KEEP * base0 + sigma * (faces(base0, 8) + timed(basep))
 
     for copy in second:
         copy.wait_recv()
@@ -400,7 +405,7 @@
                 vmem((2, 256, 128), F32), vmem((1, 256), F32), vmem((128, 128), F32), vmem((4, 128, 128), F32),
                 vmem((128, 128), F32), vmem((4, 256), jnp.int32), vmem((1, 32), jnp.int32),
                 vmem((1024, 256), BF16), vmem((256, 384), BF16), vmem((1024, 256), BF16),
-                vmem((256, 768), BF16), vmem((256, 768), BF16), vmem((256, 1024), BF16),
+                vmem((256, 768), BF16), vmem((256, 768), BF16), vmem((9, 256, 1024), BF16),
                 vmem(rows, F32), vmem((6, 32, 128), F32), vmem((5, 32, 128), F32), vmem((2, 32, 128), F32),
                 vmem(rows, F32),
                 vmem((groups, 32, 128), F32), vmem((groups, 32, 128), F32), vmem(rows, F32), vmem(rows, F32),

time: 34.1 us -> 34.1 us (level)
  no operation moved by 1% of the time
where the time goes in v6:
time: 34.1 us; the launch traced here: 34 us
  Pallas kernels  33.3 us (98%)
  local copies, waits for them, and re-layouts  0.71 us (2%)
    pallas_call x1, Pallas kernels, body(): pl.pallas_call(lambda *refs: kernel(groups, partitions, *refs), out_shape...  33.3 us
    unnamed x1, local copies, waits for them, and re-layouts  0.71 us

profile of v6, /device:TPU:1, one launch (start us, length us, event | category | flops | bytes accessed | tf_op | source)
XLA Modules:
  0.0 34.0 jit_solution(1043026888865690976)
XLA Ops:
  0.0 33.3 %shard_map.73 = f32[2,256,128]{2,1,0:T(8,128)S(1)} custom-call(f32[2,256,128]{2,1,0:T(8,128)} %refs_0_.1, f32[1,256]{1,0:T(1,128)} %bitcast.3, f32[128,128]{1,0:T(8,128)} %refs_2_.1, f32[4,128,128]{2,1,0:T(8,128)} %refs_3_.1, f32[128,128]{1,0:T(8,128)} %refs_4_.1, s32[4,256]{1,0:T(4,128)} %bitcast.2, s32[1,32]{1,0:T(1,128)} %refs_6_.1), custom_call_target="tpu_custom_call" | custom-call | tf_op jit(solution)/shard_map/pallas_call | solution.py:399
  33.3 0.7 %copy.9 = f32[2,256,128]{2,1,0:T(8,128)} copy(f32[2,256,128]{2,1,0:T(8,128)S(1)} %shard_map.73) | data formatting | bytes 524288

commit v7 on v6

--- a/solution.py
+++ b/solution.py
@@ -194,7 +194,7 @@
         remote(out1.at[1, to_left], far1.at[1, to_right], 9, {"space": space(-2)}),
     ]
     first_last = remote(v0_last, before0, 10, {"tm": after})
-    for copy in first + late + [first_last]:
+    for copy in first + [first_last]:
         copy.start()
 
     for partner in along:
@@ -248,6 +248,8 @@
     onward = coarse * (faces(onward, 4) + timed(onward) - scale * onward)
     ready = coarse * (rest0 + rest1) + base1
 
+    for copy in late:
+        copy.start()
     for copy in first:
         copy.wait_recv()
     started = k > 0

time: 34.1 us -> 34.1 us (level)
  no operation moved by 1% of the time
where the time goes in v7:
time: 34.1 us; the launch traced here: 34 us
  Pallas kernels  33.3 us (98%)
  local copies, waits for them, and re-layouts  0.71 us (2%)
    pallas_call x1, Pallas kernels, body(): pl.pallas_call(lambda *refs: kernel(groups, partitions, *refs), out_shape...  33.3 us
    unnamed x1, local copies, waits for them, and re-layouts  0.71 us

profile of v7, /device:TPU:1, one launch (start us, length us, event | category | flops | bytes accessed | tf_op | source)
XLA Modules:
  0.0 34.0 jit_solution(8145554586735962424)
XLA Ops:
  0.0 33.3 %shard_map.73 = f32[2,256,128]{2,1,0:T(8,128)S(1)} custom-call(f32[2,256,128]{2,1,0:T(8,128)} %refs_0_.1, f32[1,256]{1,0:T(1,128)} %bitcast.3, f32[128,128]{1,0:T(8,128)} %refs_2_.1, f32[4,128,128]{2,1,0:T(8,128)} %refs_3_.1, f32[128,128]{1,0:T(8,128)} %refs_4_.1, s32[4,256]{1,0:T(4,128)} %bitcast.2, s32[1,32]{1,0:T(1,128)} %refs_6_.1), custom_call_target="tpu_custom_call" | custom-call | tf_op jit(solution)/shard_map/pallas_call | solution.py:401
  33.3 0.7 %copy.9 = f32[2,256,128]{2,1,0:T(8,128)} copy(f32[2,256,128]{2,1,0:T(8,128)S(1)} %shard_map.73) | data formatting | bytes 524288
